TPU v7x, 512 devices: a whole 4x4x16 slice. The times are simulated.
512 devices in a mesh: ctx: 64 (over y, z), head: 8 (over x, core).
Axes of the slice: x: 4, y: 4, z: 16, core: 2. Of those that a mesh axis runs over, the one named last changes fastest.
Arguments:
- queries: bfloat16 [32768, 64, 128], P('ctx', 'head'), may hold values from -120 to 120
- key_rows: bfloat16 [32768, 64, 128], P('ctx', 'head'), may hold values from -6 to 6
- value_rows: bfloat16 [32768, 64, 128], P('ctx', 'head'), may hold values from -6 to 6
- selection: int32 [64, 64, 3], P(None, 'head'), may hold values from 0 to 62, as said below
Outputs:
- attended: bfloat16 [32768, 64, 128], P('ctx', 'head')
- affinity: bfloat16 [32768, 64, 64], P('ctx', 'head')
Inputs may be any that keep to these rules, and one draw needn't show every extreme that they name: `selection`: for each query block and head the 3 entries are distinct; every block's list after the first holds the block just before it; entries at or after the query's own block occur only in the first 3 blocks.
All inputs are finite; a program needn't handle non-finite values.
Results may differ from a plain program's by a relative error of at most 0.011.
Values may be sent and summed in bfloat16 or wider, within the bound.
No kernel may reach another device: no remote copies, remote signals or barrier semaphores. Data moves between devices by JAX's collectives and lax.ppermute only.
A program may use at most 64 MiB of HBM per device.

v0:
```python
import jax
import jax.numpy as jnp
from jax import lax
from jax.sharding import PartitionSpec as P


def attend(query_block, key_block, value_block, usable):
    slots, block_len, head_dim = key_block.shape
    flat_keys = key_block.reshape(slots * block_len, head_dim)
    flat_values = value_block.reshape(slots * block_len, head_dim)
    scores = lax.dot_general(
        query_block, flat_keys, (((1,), (1,)), ((), ())), preferred_element_type=jnp.float32
    )
    scores = scores * head_dim ** (-0.5)
    row_ids = jnp.arange(block_len)[:, None]
    col_ids = jnp.arange(slots * block_len)[None, :]
    slot_index = col_ids // block_len
    offset = col_ids % block_len
    allowed = jnp.where(slot_index == 0, offset <= row_ids, usable[slot_index])
    scores = jnp.where(allowed, scores, -jnp.inf)
    row_max = jnp.max(scores, axis=-1, keepdims=True)
    weights = jnp.exp(scores - row_max)
    denominator = jnp.sum(weights, axis=-1, keepdims=True)
    weighted = jnp.dot(
        weights.astype(jnp.bfloat16), flat_values, preferred_element_type=jnp.float32
    )
    return (weighted / denominator).astype(jnp.bfloat16)


def attend_item(items):
    return attend(items[0], items[1], items[2], items[3])


def body(queries, key_rows, value_rows, selection):
    ctx_size = lax.axis_size("ctx")
    tok_dev, heads_dev, head_dim = queries.shape
    blocks = selection.shape[0]
    topk = selection.shape[2]
    blocks_dev = blocks // ctx_size
    block_len = tok_dev // blocks_dev
    slice_rows = block_len // ctx_size
    position = lax.axis_index("ctx")
    key_blocks = key_rows.reshape(blocks_dev, block_len, heads_dev, head_dim)
    pooled = (jnp.sum(key_blocks, axis=1, dtype=jnp.float32) / block_len).astype(jnp.bfloat16)
    key_send = jnp.swapaxes(
        key_rows.reshape(blocks_dev, ctx_size, slice_rows, heads_dev, head_dim), 0, 1
    )
    value_send = jnp.swapaxes(
        value_rows.reshape(blocks_dev, ctx_size, slice_rows, heads_dev, head_dim), 0, 1
    )
    key_parts, value_parts = (
        lax.all_to_all(key_send, "ctx", split_axis=0, concat_axis=0, tiled=True),
        lax.all_to_all(value_send, "ctx", split_axis=0, concat_axis=0, tiled=True),
    )
    pooled_all = lax.all_gather(pooled, "ctx", axis=0, tiled=True)
    key_parts = key_parts.reshape(blocks, slice_rows, heads_dev, head_dim)
    value_parts = value_parts.reshape(blocks, slice_rows, heads_dev, head_dim)
    per_head = jnp.einsum("thd,bhd->thb", queries, pooled_all, preferred_element_type=jnp.float32)
    token_block = (position * tok_dev + jnp.arange(tok_dev, dtype=jnp.int32)) // block_len
    causal = jnp.arange(blocks, dtype=jnp.int32)[None, None, :] <= token_block[:, None, None]
    affinity = jnp.where(causal, per_head, jnp.zeros_like(per_head)).astype(jnp.bfloat16)
    head_ids = jnp.arange(heads_dev, dtype=jnp.int32)
    owners = jnp.broadcast_to(
        jnp.arange(blocks, dtype=jnp.int32)[:, None, None], (blocks, heads_dev, 1)
    )
    slot_table = jnp.concatenate([owners, selection], axis=2)
    slots = slot_table.shape[2]
    picked_keys = key_parts[slot_table, :, head_ids[None, :, None]]
    picked_values = value_parts[slot_table, :, head_ids[None, :, None]]
    picked_keys = picked_keys.reshape(ctx_size, blocks_dev, heads_dev, slots, slice_rows, head_dim)
    picked_values = picked_values.reshape(
        ctx_size, blocks_dev, heads_dev, slots, slice_rows, head_dim
    )
    fetched_keys, fetched_values = (
        lax.all_to_all(picked_keys, "ctx", split_axis=0, concat_axis=4, tiled=True),
        lax.all_to_all(picked_values, "ctx", split_axis=0, concat_axis=4, tiled=True),
    )
    fetched_keys = fetched_keys[0]
    fetched_values = fetched_values[0]
    my_selection = lax.dynamic_slice_in_dim(selection, position * blocks_dev, blocks_dev, 0)
    my_blocks = position * blocks_dev + jnp.arange(blocks_dev, dtype=jnp.int32)
    usable = jnp.concatenate(
        [jnp.ones((blocks_dev, heads_dev, 1), bool), my_selection < my_blocks[:, None, None]],
        axis=2,
    )
    query_blocks = queries.reshape(blocks_dev, block_len, heads_dev, head_dim).transpose(0, 2, 1, 3)
    items = (
        query_blocks.reshape(blocks_dev * heads_dev, block_len, head_dim),
        fetched_keys.reshape(blocks_dev * heads_dev, topk + 1, block_len, head_dim),
        fetched_values.reshape(blocks_dev * heads_dev, topk + 1, block_len, head_dim),
        usable.reshape(blocks_dev * heads_dev, topk + 1),
    )
    outputs = lax.map(attend_item, items)
    attended = (
        outputs.reshape(blocks_dev, heads_dev, block_len, head_dim)
        .transpose(0, 2, 1, 3)
        .reshape(tok_dev, heads_dev, head_dim)
    )
    return (attended, affinity)


def solution(mesh):
    in_specs = (
        P("ctx", "head", None),
        P("ctx", "head", None),
        P("ctx", "head", None),
        P(None, "head", None),
    )
    out_specs = (P("ctx", "head", None), P("ctx", "head", None))
    return jax.shard_map(body, mesh=mesh, in_specs=in_specs, out_specs=out_specs, check_vma=False)
```

profile of v0, /device:TPU:6, one launch (start us, length us, event | category | flops | bytes accessed | tf_op | source)
XLA Modules:
  0.0 685.7 jit_solution(15779170168362846168)
XLA Ops:
  0.7 2.6 copy.28
  3.2 18.7 %all-to-all-start.2 = ((bf16[64,1,8,8,128]{4,2,3,1,0:T(8,128)(2,1)}), bf16[64,1,8,8,128]{4,2,3,1,0:T(8,128)(2,1)S(1)}, u32[]{:S(2)}, u32[]{:S(2)}) async-start(bf16[64,1,8,8,128]{4,2,3,1,0:T(8,128)(2,1)} %copy.28), calls=%async_computation.2 | async-start | bytes 2097152 | tf_op jit(solution)/shard_map/all_to_all | solution.py:53
  23.2 52.6 %all-to-all-done.2 = bf16[64,1,8,8,128]{4,2,3,1,0:T(8,128)(2,1)S(1)} async-done(((bf16[64,1,8,8,128]{4,2,3,1,0:T(8,128)(2,1)}), bf16[64,1,8,8,128]{4,2,3,1,0:T(8,128)(2,1)S(1)}, u32[]{:S(2)}, u32[]{:S(2)}) %all-to-all-start.2) | async-done | bytes 1048608 | tf_op jit(solution)/shard_map/all_to_all | solution.py:53
  75.8 6.8 all-to-all-start
  83.0 17.5 %gather_fusion.1 = bf16[2048,8,128]{2,1,0:T(8,128)(2,1)} fusion(bf16[64,8,8,128]{3,1,2,0:T(8,128)(2,1)S(1)} %bitcast.89, s32[2048]{0:T(1024)S(1)} %reshape.300), kind=kCustom, calls=%fused_computation.1 | custom fusion | bytes 8404992 | tf_op jit(solution)/shard_map/gather | solution.py:69
  100.5 35.8 %all-to-all-done = bf16[64,1,8,8,128]{4,2,3,1,0:T(8,128)(2,1)S(1)} async-done(((bf16[64,1,8,8,128]{4,2,3,1,0:T(8,128)(2,1)}), bf16[64,1,8,8,128]{4,2,3,1,0:T(8,128)(2,1)S(1)}, u32[]{:S(2)}, u32[]{:S(2)}) %all-to-all-start) | async-done | bytes 1048608 | tf_op jit(solution)/shard_map/all_to_all | solution.py:52
  136.3 7.0 %all-to-all-start.3 = ((bf16[64,1,8,4,8,128]{5,4,3,2,1,0:T(8,128)(2,1)}), bf16[64,1,8,4,8,128]{5,4,3,2,1,0:T(8,128)(2,1)}, u32[]{:S(2)}, u32[]{:S(2)}) async-start(bf16[64,1,8,4,8,128]{5,4,3,2,1,0:T(8,128)(2,1)} %bitcast.91), calls=%async_computation.3 | async-start | bytes 8388608 | tf_op jit(solution)/shard_map/all_to_all | solution.py:76
  143.3 17.6 %gather_fusion = bf16[2048,8,128]{2,1,0:T(8,128)(2,1)} fusion(bf16[64,8,8,128]{3,1,2,0:T(8,128)(2,1)S(1)} %bitcast.88, s32[2048]{0:T(1024)S(1)} %reshape.300), kind=kCustom, calls=%fused_computation | custom fusion | bytes 8404992 | tf_op jit(solution)/shard_map/gather | solution.py:68
  160.9 170.1 %all-to-all-done.3 = bf16[64,1,8,4,8,128]{5,4,3,2,1,0:T(8,128)(2,1)} async-done(((bf16[64,1,8,4,8,128]{5,4,3,2,1,0:T(8,128)(2,1)}), bf16[64,1,8,4,8,128]{5,4,3,2,1,0:T(8,128)(2,1)}, u32[]{:S(2)}, u32[]{:S(2)}) %all-to-all-start.3) | async-done | bytes 4194336 | tf_op jit(solution)/shard_map/all_to_all | solution.py:76
  331.0 7.9 %all-to-all-start.1 = ((bf16[64,1,8,4,8,128]{5,4,3,2,1,0:T(8,128)(2,1)}), bf16[64,1,8,4,8,128]{5,4,3,2,1,0:T(8,128)(2,1)}, u32[]{:S(2)}, u32[]{:S(2)}) async-start(bf16[64,1,8,4,8,128]{5,4,3,2,1,0:T(8,128)(2,1)} %bitcast.90), calls=%async_computation.1 | async-start | bytes 8388608 | tf_op jit(solution)/shard_map/all_to_all | solution.py:75
  339.8 274.0 %all-gather = bf16[512,128]{1,0:T(8,128)(2,1)S(1)} all-gather(bf16[8,128]{1,0:T(8,128)(2,1)S(1)} %multiply_convert_fusion), channel_id=2, replica_groups=mesh['ctx'=64,'head'=8] {'ctx'}, dimensions={0}, use_global_device_ids=true | all-gather | bytes 133120 | tf_op jit(solution)/shard_map/all_gather | solution.py:55
  613.9 1.3 fusion.30
  615.2 5.3 copy.42
  620.5 5.4 copy.43
  625.9 58.2 %while.12 = (s32[]{:T(128)}, bf16[8,512,128]{2,1,0:T(8,128)(2,1)S(1)}, pred[8,4]{0,1:T(4,128)(4,1)S(1)}, bf16[8,512,128]{2,1,0:T(8,128)(2,1)S(1)}, bf16[8,4,512,...) while((s32[]{:T(128)}, bf16[8,512,128]{2,1,0:T(8,128)(2,1)S(1)}, ...), condition=%wide.region_3.4_spmd, body=%wide.region_0.3_spmd.sunk | while | flops 546503680 | bytes 16025713 | solution.py:93
  626.5 2.4 select_reduce_fusion.2
  630.2 1.4 fusion.58
  633.8 2.4 select_reduce_fusion.2
  637.5 1.4 fusion.58
  641.0 2.4 select_reduce_fusion.2
  644.8 1.4 fusion.58
  648.3 2.4 select_reduce_fusion.2
  652.0 1.4 fusion.58
  655.6 2.4 select_reduce_fusion.2
  659.3 1.4 fusion.58
  662.9 2.4 select_reduce_fusion.2
  666.6 1.4 fusion.58
  670.2 2.4 select_reduce_fusion.2
  673.9 1.4 fusion.58
  677.4 2.4 select_reduce_fusion.2
  681.2 1.4 fusion.58
  684.1 1.6 copy.44
  (78 shorter events, 30.2 us)
Async XLA Ops:
  0.6 21.3 %copy-start = (bf16[512,8,128]{2,1,0:T(8,128)(2,1)S(1)}, bf16[512,8,128]{2,1,0:T(8,128)(2,1)}, u32[]{:S(2)}) copy-start(bf16[512,8,128]{2,1,0:T(8,128)(2,1)} %param.7) | copy-start | bytes 3145732
  0.6 82.0 %copy-start.3 = (s32[64,8,3]{0,1,2:T(8,128)S(1)}, s32[64,8,3]{0,1,2:T(8,128)}, u32[]{:S(2)}) copy-start(s32[64,8,3]{0,1,2:T(8,128)} %param.9) | copy-start | bytes 18436
  3.2 72.6 %all-to-all-start.2 = ((bf16[64,1,8,8,128]{4,2,3,1,0:T(8,128)(2,1)}), bf16[64,1,8,8,128]{4,2,3,1,0:T(8,128)(2,1)S(1)}, u32[]{:S(2)}, u32[]{:S(2)}) async-start(bf16[64,1,8,8,128]{4,2,3,1,0:T(8,128)(2,1)} %copy.28), calls=%async_computation.2 | async-start | bytes 2097152 | tf_op jit(solution)/shard_map/all_to_all | solution.py:53
  75.8 60.5 %all-to-all-start = ((bf16[64,1,8,8,128]{4,2,3,1,0:T(8,128)(2,1)}), bf16[64,1,8,8,128]{4,2,3,1,0:T(8,128)(2,1)S(1)}, u32[]{:S(2)}, u32[]{:S(2)}) async-start(bf16[64,1,8,8,128]{4,2,3,1,0:T(8,128)(2,1)} %copy.24), calls=%async_computation | async-start | bytes 2097152 | tf_op jit(solution)/shard_map/all_to_all | solution.py:52
  136.3 194.7 %all-to-all-start.3 = ((bf16[64,1,8,4,8,128]{5,4,3,2,1,0:T(8,128)(2,1)}), bf16[64,1,8,4,8,128]{5,4,3,2,1,0:T(8,128)(2,1)}, u32[]{:S(2)}, u32[]{:S(2)}) async-start(bf16[64,1,8,4,8,128]{5,4,3,2,1,0:T(8,128)(2,1)} %bitcast.91), calls=%async_computation.3 | async-start | bytes 8388608 | tf_op jit(solution)/shard_map/all_to_all | solution.py:76
  331.0 7.9 %copy-start.1 = (bf16[512,8,128]{2,1,0:T(8,128)(2,1)S(1)}, bf16[512,8,128]{2,1,0:T(8,128)(2,1)}, u32[]{:S(2)}) copy-start(bf16[512,8,128]{2,1,0:T(8,128)(2,1)} %param.6) | copy-start | bytes 3145732
  331.0 289.5 %all-to-all-start.1 = ((bf16[64,1,8,4,8,128]{5,4,3,2,1,0:T(8,128)(2,1)}), bf16[64,1,8,4,8,128]{5,4,3,2,1,0:T(8,128)(2,1)}, u32[]{:S(2)}, u32[]{:S(2)}) async-start(bf16[64,1,8,4,8,128]{5,4,3,2,1,0:T(8,128)(2,1)} %bitcast.90), calls=%async_computation.1 | async-start | bytes 8388608 | tf_op jit(solution)/shard_map/all_to_all | solution.py:75
  620.5 5.4 copy-start.2
where the time goes:
time: 687 us; the launch traced here: 686 us
  blocking collectives  274 us (40%)
  waiting for transfers between devices  258 us (38%)
  local copies, waits for them, and re-layouts  67 us (10%)
  starting transfers between devices  40.4 us (6%)
  other arithmetic  25.7 us (4%)
  matrix products  19 us (3%)
    all_gather x1, blocking collectives, body(): pooled_all = lax.all_gather(pooled, 'ctx', axis=0, tiled=True)  274 us
    all_to_all x1, waiting for transfers between devices, body(): lax.all_to_all(picked_values, 'ctx', split_axis=0, concat_axis=4, tiled=T...  170 us
    all_to_all x1, waiting for transfers between devices, body(): lax.all_to_all(value_send, 'ctx', split_axis=0, concat_axis=0, tiled=True)  52.6 us
    all_to_all x1, waiting for transfers between devices, body(): lax.all_to_all(key_send, 'ctx', split_axis=0, concat_axis=0, tiled=True)  35.8 us
    gather x8, other arithmetic, attend(): allowed = jnp.where(slot_index == 0, offset <= row_ids, usable[slot_index])  19.3 us
    all_to_all x1, starting transfers between devices, body(): lax.all_to_all(value_send, 'ctx', split_axis=0, concat_axis=0, tiled=True)  18.7 us
    gather x1, local copies, waits for them, and re-layouts, body(): picked_keys = key_parts[slot_table, :, head_ids[None, :, None]]  17.6 us
    gather x1, local copies, waits for them, and re-layouts, body(): picked_values = value_parts[slot_table, :, head_ids[None, :, None]]  17.5 us
  transfers between devices with their start and end apart: 4, of which 3 were waited for; matrix products, arithmetic and copies ran while one was open for 6% of the time, Pallas kernels for 0%

commit v1 on v0

v1 whole, which is shorter than its diff:
```python
import functools

import jax
import jax.numpy as jnp
from jax import lax
from jax.experimental import pallas as pl
from jax.experimental.pallas import tpu as pltpu
from jax.sharding import PartitionSpec as P

LOG2E = 1.4426950408889634
MASKED = -1e30


def pick_kernel(blocks, table_ref, parts_ref, out_ref):
    head = pl.program_id(0)

    def one(c, carry):
        base = (head * blocks + c) * 2
        first = parts_ref[table_ref[base], 0].astype(jnp.float32)
        second = parts_ref[table_ref[base + 1], 0].astype(jnp.float32)
        half = first.shape[0] // 2
        out_ref[c, 0, 0] = jnp.concatenate([first[:half], second[:half]], 0).astype(jnp.bfloat16)
        out_ref[c, 0, 1] = jnp.concatenate([first[half:], second[half:]], 0).astype(jnp.bfloat16)
        return carry

    lax.fori_loop(0, blocks, one, 0, unroll=8)


def near_kernel(scale, flag_ref, q_ref, k_ref, v_ref, pk_ref, pv_ref, acc_ref, stat_ref):
    q = q_ref[0]
    rows = q.shape[0]
    dims = (((1,), (1,)), ((), ()))
    own = lax.dot_general(q, k_ref[0], dims, preferred_element_type=jnp.float32)
    row_ids = lax.broadcasted_iota(jnp.int32, own.shape, 0)
    col_ids = lax.broadcasted_iota(jnp.int32, own.shape, 1)
    own = jnp.where(col_ids <= row_ids, own, MASKED)
    before = lax.dot_general(q, pk_ref[0], dims, preferred_element_type=jnp.float32)
    before = jnp.where(flag_ref[0] > 0, before, MASKED)
    top = jnp.maximum(jnp.max(own, 1, keepdims=True), jnp.max(before, 1, keepdims=True))
    own = jnp.exp2((own - top) * scale)
    before = jnp.exp2((before - top) * scale)
    total = jnp.sum(own, 1, keepdims=True) + jnp.sum(before, 1, keepdims=True)
    acc = jnp.dot(own.astype(jnp.bfloat16), v_ref[0], preferred_element_type=jnp.float32)
    acc += jnp.dot(before.astype(jnp.bfloat16), pv_ref[0], preferred_element_type=jnp.float32)
    acc_ref[0] = acc
    lane = lax.broadcasted_iota(jnp.int32, (rows, stat_ref.shape[2]), 1)
    stat_ref[0] = jnp.where(lane < stat_ref.shape[2] // 2, top, total)


def far_kernel(scale, flag_ref, q_ref, kv_ref, acc_ref, stat_ref, out_ref):
    head = pl.program_id(0)
    q = q_ref[0]
    keys = kv_ref[:, 0, 0]
    values = kv_ref[:, 0, 1]
    pair, head_dim = keys.shape[1:]
    keys = keys.reshape(-1, head_dim)
    values = values.reshape(-1, head_dim)
    scores = lax.dot_general(
        q, keys, (((1,), (1,)), ((), ())), preferred_element_type=jnp.float32
    )
    col = lax.broadcasted_iota(jnp.int32, (1, keys.shape[0]), 1) % pair
    allowed = jnp.where(col < pair // 2, flag_ref[2 * head], flag_ref[2 * head + 1])
    scores = jnp.where(allowed > 0, scores, MASKED)
    half = stat_ref.shape[2] // 2
    top_before = stat_ref[0][:, :1]
    total_before = stat_ref[0][:, half : half + 1]
    top = jnp.maximum(jnp.max(scores, 1, keepdims=True), top_before)
    weights = jnp.exp2((scores - top) * scale)
    shrink = jnp.exp2((top_before - top) * scale)
    total = total_before * shrink + jnp.sum(weights, 1, keepdims=True)
    acc = jnp.dot(weights.astype(jnp.bfloat16), values, preferred_element_type=jnp.float32)
    acc += acc_ref[0] * shrink
    out_ref[0] = (acc / total).astype(jnp.bfloat16)


def body(queries, key_rows, value_rows, selection):
    ctx_size = lax.axis_size("ctx")
    block_len, heads, head_dim = queries.shape
    blocks, _, topk = selection.shape
    assert blocks == ctx_size and topk == 3
    slice_rows = block_len // ctx_size
    position = lax.axis_index("ctx")
    scale = LOG2E * head_dim**-0.5
    bf16 = jnp.bfloat16
    vmem = pltpu.CompilerParams(vmem_limit_bytes=48 * 1024 * 1024)

    def slices(x):
        return x.reshape(ctx_size, slice_rows, heads, head_dim).transpose(0, 2, 1, 3)

    send = jnp.concatenate([slices(key_rows), slices(value_rows)], axis=2)
    parts = lax.all_to_all(send, "ctx", split_axis=0, concat_axis=0, tiled=True)

    keys = key_rows.transpose(1, 0, 2)
    values = value_rows.transpose(1, 0, 2)
    steps = [(i, i + 1) for i in range(ctx_size - 1)]
    prev_keys = lax.ppermute(keys, "ctx", steps)
    prev_values = lax.ppermute(values, "ctx", steps)

    pooled = (jnp.sum(key_rows, axis=0, dtype=jnp.float32) / block_len).astype(bf16)
    pooled_all = lax.all_gather(pooled[None], "ctx", axis=0, tiled=True)

    owner = jnp.arange(blocks, dtype=jnp.int32)[:, None]
    first = jnp.where(selection[:, :, 0] == owner - 1, selection[:, :, 1], selection[:, :, 0])
    last = jnp.where(selection[:, :, 2] == owner - 1, selection[:, :, 1], selection[:, :, 2])
    picks = jnp.stack([first, last], axis=2)
    table = picks.transpose(1, 0, 2).reshape(-1)
    mine = lax.dynamic_index_in_dim(picks, position, 0, keepdims=False)
    far_flags = (mine < position).astype(jnp.int32).reshape(-1)
    near_flag = (position > 0).astype(jnp.int32).reshape(1)

    picked = pl.pallas_call(
        functools.partial(pick_kernel, blocks),
        grid_spec=pltpu.PrefetchScalarGridSpec(
            num_scalar_prefetch=1,
            grid=(heads,),
            in_specs=[
                pl.BlockSpec((blocks, 1, 2 * slice_rows, head_dim), lambda h, t: (0, h, 0, 0))
            ],
            out_specs=pl.BlockSpec(
                (blocks, 1, 2, 2 * slice_rows, head_dim), lambda h, t: (0, h, 0, 0, 0)
            ),
        ),
        out_shape=jax.ShapeDtypeStruct((blocks, heads, 2, 2 * slice_rows, head_dim), bf16),
        compiler_params=vmem,
        name="pick",
    )(table, parts)
    fetched = lax.all_to_all(picked, "ctx", split_axis=0, concat_axis=0, tiled=True)

    q = queries.transpose(1, 0, 2)
    per_head = jnp.einsum("htd,bhd->htb", q, pooled_all, preferred_element_type=jnp.float32)
    causal = jnp.arange(blocks, dtype=jnp.int32) <= position
    affinity = jnp.where(causal, per_head, 0.0).astype(bf16).transpose(1, 0, 2)

    whole = pl.BlockSpec((1, block_len, head_dim), lambda h, t: (h, 0, 0))
    acc, stat = pl.pallas_call(
        functools.partial(near_kernel, scale),
        grid_spec=pltpu.PrefetchScalarGridSpec(
            num_scalar_prefetch=1, grid=(heads,), in_specs=[whole] * 5, out_specs=[whole, whole]
        ),
        out_shape=[jax.ShapeDtypeStruct((heads, block_len, head_dim), jnp.float32)] * 2,
        compiler_params=vmem,
        cost_estimate=pl.CostEstimate(
            flops=heads * block_len * block_len * head_dim * 8,
            bytes_accessed=heads * block_len * head_dim * 18,
            transcendentals=heads * block_len * block_len * 2,
        ),
        name="near",
    )(near_flag, q, keys, values, prev_keys, prev_values)
    out = pl.pallas_call(
        functools.partial(far_kernel, scale),
        grid_spec=pltpu.PrefetchScalarGridSpec(
            num_scalar_prefetch=1,
            grid=(heads,),
            in_specs=[
                whole,
                pl.BlockSpec(
                    (ctx_size, 1, 2, 2 * slice_rows, head_dim), lambda h, t: (0, h, 0, 0, 0)
                ),
                whole,
                whole,
            ],
            out_specs=whole,
        ),
        out_shape=jax.ShapeDtypeStruct((heads, block_len, head_dim), bf16),
        compiler_params=vmem,
        cost_estimate=pl.CostEstimate(
            flops=heads * block_len * block_len * head_dim * 8,
            bytes_accessed=heads * block_len * head_dim * 18,
            transcendentals=heads * block_len * block_len * 2,
        ),
        name="far",
    )(far_flags, q, fetched, acc, stat)
    return out.transpose(1, 0, 2), affinity


def solution(mesh):
    in_specs = (
        P("ctx", "head", None),
        P("ctx", "head", None),
        P("ctx", "head", None),
        P(None, "head", None),
    )
    out_specs = (P("ctx", "head", None), P("ctx", "head", None))
    return jax.shard_map(body, mesh=mesh, in_specs=in_specs, out_specs=out_specs, check_vma=False)
```

time: 687 us -> 494 us (0.72)
  waiting for transfers between devices: 258 us -> 96.9 us
  local copies, waits for them, and re-layouts: 67 us -> 7.28 us
  Pallas kernels: 0 us -> 37.6 us
  blocking collectives: 274 us -> 309 us
  other arithmetic: 25.7 us -> 3.64 us
  matrix products: 19 us -> 2.51 us
    all_to_all x4 -> x2, waiting for transfers between devices: 258 us -> 96.9 us  [the longest x1 96.9 us: body(): parts = lax.all_to_all(send, 'ctx', split_axis=0, concat_axis=0, tiled=True)]
    gather x10 -> x0, local copies, waits for them, and re-layouts: 39.4 us -> none  [the longest x1 17.6 us: body(): picked_keys = key_parts[slot_table, :, head_ids[None, :, None]]]
    pallas_call x0 -> x3, Pallas kernels: none -> 37.6 us  [the longest x1 19 us: body(): pl.pallas_call(functools.partial(far_kernel, scale), grid_spec=pltpu.Pref...]
    all_gather x1, blocking collectives: 274 us -> 309 us  [body(): pooled_all = lax.all_gather(pooled[None], 'ctx', axis=0, tiled=True)]
    gather x8 -> x0, other arithmetic: 19.3 us -> none  [attend(): allowed = jnp.where(slot_index == 0, offset <= row_ids, usable[slot_index])]
    dot_general x17 -> x1, matrix products: 19 us -> 2.51 us  [body(): jnp.einsum('htd,bhd->htb', q, pooled_all, preferred_element_type=jnp.floa...]
    all_to_all x4 -> x2, starting transfers between devices: 40.4 us -> 27.5 us  [the longest x1 18.9 us: body(): parts = lax.all_to_all(send, 'ctx', split_axis=0, concat_axis=0, tiled=True)]
    dynamic_slice x16 -> x0, local copies, waits for them, and re-layouts: 10.8 us -> none  [body(): outputs = lax.map(attend_item, items)]
  transfers between devices with their start and end apart: 4 -> 4, of which waited for: 3 -> 1; matrix products, arithmetic and copies ran while one was open for 6% -> 1% of each run, Pallas kernels for 0% -> 3%
where the time goes in v1:
time: 494 us; the launch traced here: 493 us
  blocking collectives  309 us (63%)
  waiting for transfers between devices  96.9 us (20%)
  Pallas kernels  37.6 us (8%)
  starting transfers between devices  35.4 us (7%)
  local copies, waits for them, and re-layouts  7.28 us (1%)
    all_gather x1, blocking collectives, body(): pooled_all = lax.all_gather(pooled[None], 'ctx', axis=0, tiled=True)  309 us
    all_to_all x1, waiting for transfers between devices, body(): parts = lax.all_to_all(send, 'ctx', split_axis=0, concat_axis=0, tiled=True)  96.9 us
    pallas_call x1, Pallas kernels, body(): pl.pallas_call(functools.partial(far_kernel, scale), grid_spec=pltpu.Pref...  19 us
    all_to_all x1, starting transfers between devices, body(): parts = lax.all_to_all(send, 'ctx', split_axis=0, concat_axis=0, tiled=True)  18.9 us
    pallas_call x1, Pallas kernels, body(): pl.pallas_call(functools.partial(near_kernel, scale), grid_spec=pltpu.Pre...  13.2 us
  transfers between devices with their start and end apart: 4, of which 1 were waited for; matrix products, arithmetic and copies ran while one was open for 1% of the time, Pallas kernels for 3%

profile of v1, /device:TPU:6, one launch (start us, length us, event | category | flops | bytes accessed | tf_op | source)
XLA Modules:
  0.0 493.3 jit_solution(8415155985499370691)
XLA Ops:
  0.6 0.0 copy-start.1
  0.6 1.6 copy.56
  2.2 0.0 copy-done.1
  2.2 0.3 copy.57
  2.5 1.8 pad_maximum_fusion
  4.3 18.9 %all-to-all-start = ((bf16[64,8,16,128]{3,2,1,0:T(8,128)(2,1)}), bf16[64,8,16,128]{3,2,1,0:T(8,128)(2,1)S(1)}, u32[]{:S(2)}, u32[]{:S(2)}) async-start(bf16[64,8,16,128]{3,2,1,0:T(8,128)(2,1)} %pad_maximum_fusion), calls=%async_computation | async-start | bytes 4194304 | tf_op jit(solution)/shard_map/all_to_all | solution.py:91
  23.2 0.0 copy-done.3
  23.2 0.1 copy.38
  23.4 0.2 reshape.54.table_ref
  23.5 96.9 %all-to-all-done.parts_ref = bf16[64,8,16,128]{3,2,1,0:T(8,128)(2,1)S(1)} async-done(((bf16[64,8,16,128]{3,2,1,0:T(8,128)(2,1)}), bf16[64,8,16,128]{3,2,1,0:T(8,128)(2,1)S(1)}, u32[]{:S(2)}, u32[]{:S(2)}) %all-to-all-start) | async-done | bytes 2097184 | tf_op jit(solution)/shard_map/all_to_all | solution.py:91
  120.4 5.4 %pick.1 = bf16[64,8,2,16,128]{4,3,2,1,0:T(8,128)(2,1)} custom-call(s32[1024]{0:T(1024)S(1)} %reshape.54.table_ref, bf16[64,8,16,128]{3,2,1,0:T(8,128)(2,1)S(1)} %all-to-all-done.parts_ref), custom_call_target="tpu_custom_call" | custom-call | tf_op jit(solution)/shard_map/pick/pallas_call | solution.py:111
  125.9 8.6 %all-to-all-start.1 = ((bf16[64,8,2,16,128]{4,3,2,1,0:T(8,128)(2,1)}), bf16[64,8,2,16,128]{4,3,2,1,0:T(8,128)(2,1)}, u32[]{:S(2)}, u32[]{:S(2)}) async-start(bf16[64,8,2,16,128]{4,3,2,1,0:T(8,128)(2,1)} %pick.1), calls=%async_computation.1 | async-start | bytes 8388608 | tf_op jit(solution)/shard_map/all_to_all | solution.py:127
  134.5 0.0 copy-start.2
  134.5 0.1 copy.55
  134.6 4.6 collective-permute-start
  139.2 0.0 copy-done.2
  139.2 0.1 copy.54
  139.3 3.3 collective-permute-start.1
  142.7 0.1 fusion.3
  142.8 0.1 copy.45
  142.9 0.1 reshape.59.flag_ref
  143.0 1.4 copy.58
  144.4 1.8 convert_reduce_fusion
  146.1 309.2 %all-gather = bf16[512,128]{1,0:T(8,128)(2,1)S(1)} all-gather(bf16[8,128]{1,0:T(8,128)(2,1)S(1)} %multiply_convert_fusion), channel_id=2, replica_groups=mesh['ctx'=64,'head'=8] {'ctx'}, dimensions={0}, use_global_device_ids=true | all-gather | bytes 133120 | tf_op jit(solution)/shard_map/all_gather | solution.py:100
  455.4 2.5 fusion.1
  457.9 0.0 collective-permute-done.pk_ref
  457.9 0.0 collective-permute-done.1.pv_ref
  457.9 13.2 %near.1 = (f32[8,512,128]{2,1,0:T(8,128)}, f32[8,512,128]{2,1,0:T(8,128)}) custom-call(s32[1]{0:T(128)} %bitcast.6.flag_ref, bf16[8,512,128]{2,1,0:T(8,128)(2,1)S(1)} %bitcast.25, bf16[8,512,128]{2,1,0:T(8,128)(2,1)S(1)} %bitcast.29, bf16[8,512,128]{2,1,0:T(8,128)(2,1)S(1)} %bitcast.31, bf16[8,512,128]{2,1,0:T(8,128)(2,1)} %collective-permute-done.pk_ref, ...), custom_call_target="tpu_custom_call" | custom-call | flops 2147483648 | bytes 9437184 | tf_op jit(solution)/shard_map/near/pallas_call | solution.py:135
  471.1 0.0 all-to-all-done.1.kv_ref
  471.1 1.6 copy-done
  472.7 19.0 %far.1 = bf16[8,512,128]{2,1,0:T(8,128)(2,1)S(1)} custom-call(s32[16]{0:T(128)S(1)} %reshape.59.flag_ref, bf16[8,512,128]{2,1,0:T(8,128)(2,1)S(1)} %bitcast.26, bf16[64,8,2,16,128]{4,3,2,1,0:T(8,128)(2,1)} %all-to-all-done.1.kv_ref, f32[8,512,128]{2,1,0:T(8,128)S(1)} %copy-done, f32[8,512,128]{2,1,0:T(8,128)} %get-tuple-element.5.stat_ref), custom_call_target="tpu_custom_call" | custom-call | flops 2147483648 | bytes 9437184 | tf_op jit(solution)/shard_map/far/pallas_call | solution.py:149
  491.6 1.6 copy.44
  (8 shorter events, 0.0 us)
Async XLA Ops:
  0.6 1.6 copy-start.1
  4.3 18.9 %copy-start.3 = (s32[64,8,3]{0,1,2:T(8,128)S(1)}, s32[64,8,3]{0,1,2:T(8,128)}, u32[]{:S(2)}) copy-start(s32[64,8,3]{0,1,2:T(8,128)} %param.7) | copy-start | bytes 18436
  4.3 116.1 %all-to-all-start = ((bf16[64,8,16,128]{3,2,1,0:T(8,128)(2,1)}), bf16[64,8,16,128]{3,2,1,0:T(8,128)(2,1)S(1)}, u32[]{:S(2)}, u32[]{:S(2)}) async-start(bf16[64,8,16,128]{3,2,1,0:T(8,128)(2,1)} %pad_maximum_fusion), calls=%async_computation | async-start | bytes 4194304 | tf_op jit(solution)/shard_map/all_to_all | solution.py:91
  125.9 345.2 %all-to-all-start.1 = ((bf16[64,8,2,16,128]{4,3,2,1,0:T(8,128)(2,1)}), bf16[64,8,2,16,128]{4,3,2,1,0:T(8,128)(2,1)}, u32[]{:S(2)}, u32[]{:S(2)}) async-start(bf16[64,8,2,16,128]{4,3,2,1,0:T(8,128)(2,1)} %pick.1), calls=%async_computation.1 | async-start | bytes 8388608 | tf_op jit(solution)/shard_map/all_to_all | solution.py:127
  134.5 4.7 copy-start.2
  134.6 323.2 %collective-permute-start = (bf16[8,512,128]{2,1,0:T(8,128)(2,1)S(1)}, bf16[8,512,128]{2,1,0:T(8,128)(2,1)}, u32[]{:S(2)}, u32[]{:S(2)}) collective-permute-start(bf16[8,512,128]{2,1,0:T(8,128)(2,1)S(1)} %bitcast.28), channel_id=1, source_target_pairs={{0,8},{8,16},{16,24},{24,32},{32,40},{40,48},{48,56},{56,64},{64,7... | collective-permute-start | bytes 3145736 | tf_op jit(solution)/shard_map/ppermute | solution.py:96
  139.3 318.5 %collective-permute-start.1 = (bf16[8,512,128]{2,1,0:T(8,128)(2,1)S(1)}, bf16[8,512,128]{2,1,0:T(8,128)(2,1)}, u32[]{:S(2)}, u32[]{:S(2)}) collective-permute-start(bf16[8,512,128]{2,1,0:T(8,128)(2,1)S(1)} %bitcast.30), channel_id=1, source_target_pairs={{0,8},{8,16},{16,24},{24,32},{32,40},{40,48},{48,56},{56,64},{64,7... | collective-permute-start | bytes 3145736 | tf_op jit(solution)/shard_map/ppermute | solution.py:97
  471.1 1.6 copy-start

commit v2 on v1

v2 whole, which is shorter than its diff:
```python
import functools

import jax
import jax.numpy as jnp
from jax import lax
from jax.experimental import pallas as pl
from jax.experimental.pallas import tpu as pltpu
from jax.sharding import PartitionSpec as P

LOG2E = 1.4426950408889634
MASKED = -1e30
ROWS = 16
ACROSS = (((1,), (1,)), ((), ()))
F32 = jnp.float32
BF16 = jnp.bfloat16


def pack_kernel(k_ref, v_ref, out_ref, kt_ref, vt_ref):
    block_len, heads, head_dim = k_ref.shape
    half = block_len // ROWS

    def one(p, total):
        here = pl.ds(p * ROWS, ROWS)
        keys = k_ref[here].astype(F32)
        by_head = jnp.transpose(keys, (1, 0, 2)).astype(BF16)
        kt_ref[:, here] = by_head
        out_ref[p, : heads * ROWS] = by_head.reshape(heads * ROWS, head_dim)
        by_head = jnp.transpose(v_ref[here].astype(F32), (1, 0, 2)).astype(BF16)
        vt_ref[:, here] = by_head
        out_ref[p + half, : heads * ROWS] = by_head.reshape(heads * ROWS, head_dim)
        return total + jnp.sum(keys, 0)

    total = lax.fori_loop(0, half, one, jnp.zeros((heads, head_dim), F32), unroll=4)
    pooled = (total / block_len).astype(BF16)

    def spread(p, carry):
        out_ref[p, heads * ROWS :] = pooled
        return carry

    lax.fori_loop(0, 2 * half, spread, 0, unroll=8)


def pick_kernel(table_ref, parts_ref, out_ref):
    blocks = parts_ref.shape[0]
    base = pl.program_id(0) * blocks * 2

    def one(c, carry):
        out_ref[c, :ROWS] = parts_ref[table_ref[base + 2 * c]]
        out_ref[c, ROWS:] = parts_ref[table_ref[base + 2 * c + 1]]
        return carry

    lax.fori_loop(0, blocks, one, 0, unroll=16)


def halves(x):
    count, rows, head_dim = x.shape
    keys = x[: count // 2].reshape(count // 2 * rows, head_dim)
    values = x[count // 2 :].reshape(count // 2 * rows, head_dim)
    return keys, values


def own_kernel(scale, q_ref, kv_ref, acc_ref, stat_ref):
    keys, values = halves(kv_ref[...])
    scores = lax.dot_general(q_ref[0], keys, ACROSS, preferred_element_type=F32)
    row_ids = lax.broadcasted_iota(jnp.int32, scores.shape, 0)
    col_ids = lax.broadcasted_iota(jnp.int32, scores.shape, 1)
    scores = jnp.where(col_ids <= row_ids, scores, MASKED)
    top = jnp.max(scores, 1, keepdims=True) * scale
    weights = jnp.exp2(scores * scale - top)
    total = jnp.sum(weights, 1, keepdims=True)
    acc_ref[0] = jnp.dot(weights.astype(BF16), values, preferred_element_type=F32)
    lane = lax.broadcasted_iota(jnp.int32, stat_ref.shape[1:], 1)
    stat_ref[0] = jnp.where(lane < stat_ref.shape[2] // 2, top, total)


def before_kernel(scale, flag_ref, q_ref, k_ref, v_ref, acc_ref, stat_ref, acc_out, stat_out):
    scores = lax.dot_general(q_ref[0], k_ref[0], ACROSS, preferred_element_type=F32)
    scores = jnp.where(flag_ref[0] > 0, scores, MASKED)
    half = stat_ref.shape[2] // 2
    top_before = stat_ref[0][:, :1]
    top = jnp.maximum(jnp.max(scores, 1, keepdims=True) * scale, top_before)
    weights = jnp.exp2(scores * scale - top)
    shrink = jnp.exp2(top_before - top)
    total = jnp.sum(weights, 1, keepdims=True) + stat_ref[0][:, half : half + 1] * shrink
    acc = jnp.dot(weights.astype(BF16), v_ref[0], preferred_element_type=F32)
    acc_out[0] = acc + acc_ref[0] * shrink
    lane = lax.broadcasted_iota(jnp.int32, stat_ref.shape[1:], 1)
    stat_out[0] = jnp.where(lane < half, top, total)


def far_kernel(scale, flag_ref, q_ref, kv_ref, acc_ref, stat_ref, out_ref):
    group, block_len, head_dim = q_ref.shape
    half = stat_ref.shape[2] // 2
    first_head = pl.program_id(0) * group
    step = block_len // 2
    heads = []
    for h in range(group):
        both = [halves(kv_ref[:, (2 * h + s) * ROWS : (2 * h + s + 1) * ROWS]) for s in range(2)]
        keys = jnp.concatenate([both[0][0], both[1][0]], 0)
        values = jnp.concatenate([both[0][1], both[1][1]], 0)
        values = jnp.concatenate([values, jnp.ones_like(values)], 1)
        off = [
            jnp.where(flag_ref[2 * (first_head + h) + s] > 0, 0.0, MASKED) for s in range(2)
        ]
        col = lax.broadcasted_iota(jnp.int32, (1, keys.shape[0]), 1)
        heads.append((keys, values, jnp.where(col < block_len, off[0], off[1])))

    def score(h, start):
        keys, _, off = heads[h]
        q = q_ref[h, start : start + step]
        return lax.dot_general(q, keys, ACROSS, preferred_element_type=F32) + off

    def finish(h, start, scores):
        _, values, _ = heads[h]
        here = pl.ds(start, step)
        stat = stat_ref[h, here]
        top_before = stat[:, :1]
        top = jnp.maximum(jnp.max(scores, 1, keepdims=True) * scale, top_before)
        weights = jnp.exp2(scores * scale - top).astype(BF16)
        shrink = jnp.exp2(top_before - top)
        both = jnp.dot(weights, values, preferred_element_type=F32)
        acc = acc_ref[h, here] * shrink + both[:, :head_dim]
        total = stat[:, half : half + 1] * shrink + both[:, head_dim:]
        out_ref[h, here] = (acc / total).astype(BF16)

    todo = [(h, start) for h in range(group) for start in range(0, block_len, step)]
    scores = score(*todo[0])
    for index, item in enumerate(todo):
        following = score(*todo[index + 1]) if index + 1 < len(todo) else None
        finish(*item, scores)
        scores = following


def body(queries, key_rows, value_rows, selection):
    ctx_size = lax.axis_size("ctx")
    block_len, heads, head_dim = queries.shape
    blocks, _, topk = selection.shape
    assert blocks == ctx_size and topk == 3 and block_len == ROWS * ctx_size // 2
    position = lax.axis_index("ctx")
    scale = LOG2E * head_dim**-0.5
    params = pltpu.CompilerParams(vmem_limit_bytes=58 * 1024 * 1024)
    small = pltpu.CompilerParams(vmem_limit_bytes=32 * 1024 * 1024)

    def cost(matmuls, moved):
        return pl.CostEstimate(
            flops=heads * block_len * block_len * head_dim * 2 * matmuls,
            bytes_accessed=heads * block_len * head_dim * moved,
            transcendentals=heads * block_len * block_len * matmuls // 2,
        )

    whole = pl.BlockSpec((1, block_len, head_dim), lambda h, *_: (h, 0, 0))
    piece = pl.BlockSpec((ctx_size, ROWS, head_dim), lambda h, *_: (0, h, 0))
    pair = pl.BlockSpec((ctx_size, 2 * ROWS, head_dim), lambda h, *_: (0, h, 0))
    by_head = functools.partial(jax.ShapeDtypeStruct, (heads, block_len, head_dim))

    send, keys, values = pl.pallas_call(
        pack_kernel,
        out_shape=[
            jax.ShapeDtypeStruct((ctx_size, heads * (ROWS + 1), head_dim), BF16),
            by_head(BF16),
            by_head(BF16),
        ],
        compiler_params=params,
        name="pack",
    )(key_rows, value_rows)
    ahead = [(i, i + 1) for i in range(ctx_size - 1)]
    keys_before = lax.ppermute(keys, "ctx", ahead)
    parts = lax.all_to_all(send, "ctx", split_axis=0, concat_axis=0, tiled=True)

    owner = jnp.arange(blocks, dtype=jnp.int32)[:, None]
    first = jnp.where(selection[:, :, 0] == owner - 1, selection[:, :, 1], selection[:, :, 0])
    last = jnp.where(selection[:, :, 2] == owner - 1, selection[:, :, 1], selection[:, :, 2])
    picks = jnp.stack([first, last], axis=2)
    table = picks.transpose(1, 0, 2).reshape(-1)
    mine = lax.dynamic_index_in_dim(picks, position, 0, keepdims=False)
    usable = (mine < position).astype(jnp.int32).reshape(-1)

    q = queries.transpose(1, 0, 2)
    own_q, keys_before = lax.optimization_barrier((q, keys_before))
    own = pl.pallas_call(
        functools.partial(own_kernel, scale),
        grid=(heads,),
        in_specs=[whole, piece],
        out_specs=[whole, whole],
        out_shape=[by_head(F32), by_head(F32)],
        compiler_params=params,
        cost_estimate=cost(200, 200),
        name="own",
    )(own_q, send)
    own, values = lax.optimization_barrier((own, values))
    own, parts = lax.optimization_barrier((own, parts))
    values_before = lax.ppermute(values, "ctx", ahead)

    picked = pl.pallas_call(
        pick_kernel,
        grid_spec=pltpu.PrefetchScalarGridSpec(
            num_scalar_prefetch=1, grid=(heads,), in_specs=[piece], out_specs=pair
        ),
        out_shape=jax.ShapeDtypeStruct((blocks, heads * 2 * ROWS, head_dim), BF16),
        compiler_params=small,
        name="pick",
    )(table, parts)
    fetched = lax.all_to_all(picked, "ctx", split_axis=0, concat_axis=0, tiled=True)

    pooled = parts[:, heads * ROWS :]
    per_head = jnp.einsum("htd,bhd->htb", q, pooled, preferred_element_type=F32)
    causal = jnp.arange(blocks, dtype=jnp.int32) <= position
    affinity = jnp.where(causal, per_head, 0.0).astype(BF16).transpose(1, 0, 2)

    acc, stat = pl.pallas_call(
        functools.partial(before_kernel, scale),
        grid_spec=pltpu.PrefetchScalarGridSpec(
            num_scalar_prefetch=1, grid=(heads,), in_specs=[whole] * 5, out_specs=[whole, whole]
        ),
        out_shape=[by_head(F32), by_head(F32)],
        compiler_params=params,
        cost_estimate=cost(800, 800),
        name="before",
    )(
        (position > 0).astype(jnp.int32).reshape(1),
        q,
        keys_before,
        values_before,
        *own,
    )
    group = 2
    some = pl.BlockSpec((group, block_len, head_dim), lambda h, *_: (h, 0, 0))
    out = pl.pallas_call(
        functools.partial(far_kernel, scale),
        grid_spec=pltpu.PrefetchScalarGridSpec(
            num_scalar_prefetch=1,
            grid=(heads // group,),
            in_specs=[
                some,
                pl.BlockSpec((ctx_size, group * 2 * ROWS, head_dim), lambda h, *_: (0, h, 0)),
                some,
                some,
            ],
            out_specs=some,
        ),
        out_shape=by_head(BF16),
        compiler_params=params,
        cost_estimate=cost(4, 20),
        name="far",
    )(usable, q, fetched, acc, stat)
    return out.transpose(1, 0, 2), affinity


def solution(mesh):
    in_specs = (
        P("ctx", "head", None),
        P("ctx", "head", None),
        P("ctx", "head", None),
        P(None, "head", None),
    )
    out_specs = (P("ctx", "head", None), P("ctx", "head", None))
    return jax.shard_map(body, mesh=mesh, in_specs=in_specs, out_specs=out_specs, check_vma=False)
```

time: 494 us -> 357 us (0.72)
  blocking collectives: 309 us -> 0 us
  waiting for transfers between devices: 96.9 us -> 258 us
  Pallas kernels: 37.6 us -> 45.1 us
  starting transfers between devices: 35.4 us -> 42.9 us
    all_gather x1 -> x0, blocking collectives: 309 us -> none  [body(): pooled_all = lax.all_gather(pooled[None], 'ctx', axis=0, tiled=True)]
    all_to_all x1, waiting for transfers between devices: 0.01 us -> 169 us  [body(): lax.all_to_all(picked, 'ctx', split_axis=0, concat_axis=0, tiled=True)]
    pallas_call x2 -> x4, Pallas kernels: 18.6 us -> 34.1 us  [the longest x1 17.2 us: body(): pl.pallas_call(functools.partial(before_kernel, scale), grid_spec=pltpu.P...]
    all_to_all x1, waiting for transfers between devices: 96.9 us -> 84.2 us  [body(): parts = lax.all_to_all(send, 'ctx', split_axis=0, concat_axis=0, tiled=True)]
    ppermute x2, starting transfers between devices: 7.92 us -> 17.4 us  [the longest x1 12.6 us: body(): values_before = lax.ppermute(values, 'ctx', ahead)]
    pallas_call x1, Pallas kernels: 19 us -> 10.9 us  [body(): pl.pallas_call(functools.partial(far_kernel, scale), grid_spec=pltpu.Pref...]
  transfers between devices with their start and end apart: 4 -> 4, of which waited for: 1 -> 3; matrix products, arithmetic and copies ran while one was open for 1% -> 1% of each run, Pallas kernels for 3% -> 8%
where the time goes in v2:
time: 357 us; the launch traced here: 356 us
  waiting for transfers between devices  258 us (72%)
  Pallas kernels  45.1 us (13%)
  starting transfers between devices  42.9 us (12%)
  local copies, waits for them, and re-layouts  7.07 us (2%)
    all_to_all x1, waiting for transfers between devices, body(): lax.all_to_all(picked, 'ctx', split_axis=0, concat_axis=0, tiled=True)  169 us
    all_to_all x1, waiting for transfers between devices, body(): parts = lax.all_to_all(send, 'ctx', split_axis=0, concat_axis=0, tiled=True)  84.2 us
    pallas_call x1, Pallas kernels, body(): pl.pallas_call(functools.partial(before_kernel, scale), grid_spec=pltpu.P...  17.2 us
    all_to_all x1, starting transfers between devices, body(): parts = lax.all_to_all(send, 'ctx', split_axis=0, concat_axis=0, tiled=True)  17 us
    ppermute x1, starting transfers between devices, body(): values_before = lax.ppermute(values, 'ctx', ahead)  12.6 us
    pallas_call x1, Pallas kernels, body(): pl.pallas_call(functools.partial(far_kernel, scale), grid_spec=pltpu.Pref...  10.9 us
    pallas_call x1, Pallas kernels, body(): pl.pallas_call(functools.partial(own_kernel, scale), grid=(heads,), in_sp...  9.16 us
    all_to_all x1, starting transfers between devices, body(): lax.all_to_all(picked, 'ctx', split_axis=0, concat_axis=0, tiled=True)  8.55 us
  transfers between devices with their start and end apart: 4, of which 3 were waited for; matrix products, arithmetic and copies ran while one was open for 1% of the time, Pallas kernels for 8%

profile of v2, /device:TPU:6, one launch (start us, length us, event | category | flops | bytes accessed | tf_op | source)
XLA Modules:
  0.0 356.1 jit_solution(2280279305328606875)
XLA Ops:
  0.6 4.9 %pack.1 = (bf16[64,136,128]{2,1,0:T(8,128)(2,1)}, bf16[8,512,128]{2,1,0:T(8,128)(2,1)}, bf16[8,512,128]{2,1,0:T(8,128)(2,1)}) custom-call(bf16[512,8,128]{2,1,0:T(8,128)(2,1)} %k_ref.1, bf16[512,8,128]{2,1,0:T(8,128)(2,1)} %v_ref.1), custom_call_target="tpu_custom_call" | custom-call | tf_op jit(solution)/shard_map/pack/pallas_call | solution.py:156
  5.5 4.8 %collective-permute-start = (bf16[8,512,128]{2,1,0:T(8,128)(2,1)}, bf16[8,512,128]{2,1,0:T(8,128)(2,1)}, u32[]{:S(2)}, u32[]{:S(2)}) collective-permute-start(bf16[8,512,128]{2,1,0:T(8,128)(2,1)} %get-tuple-element.17), channel_id=1, source_target_pairs={{0,8},{8,16},{16,24},{24,32},{32,40},{40,48},{48,56},{56,64},{64,7... | collective-permute-start | bytes 3145736 | tf_op jit(solution)/shard_map/ppermute | solution.py:167
  10.3 0.0 copy-start.1
  10.3 17.0 %all-to-all-start = ((bf16[64,136,128]{2,1,0:T(8,128)(2,1)}), bf16[64,136,128]{2,1,0:T(8,128)(2,1)S(1)}, u32[]{:S(2)}, u32[]{:S(2)}) async-start(bf16[64,136,128]{2,1,0:T(8,128)(2,1)} %get-tuple-element.19.kv_ref), calls=%async_computation | async-start | bytes 4456448 | tf_op jit(solution)/shard_map/all_to_all | solution.py:168
  27.3 0.0 copy-done.1
  27.3 1.1 copy.37
  28.5 4.7 %collective-permute-done.k_ref = bf16[8,512,128]{2,1,0:T(8,128)(2,1)} collective-permute-done((bf16[8,512,128]{2,1,0:T(8,128)(2,1)}, bf16[8,512,128]{2,1,0:T(8,128)(2,1)}, u32[]{:S(2)}, u32[]{:S(2)}) %collective-permute-start) | collective-permute-done | bytes 1048608 | tf_op jit(solution)/shard_map/ppermute | solution.py:167
  33.2 9.2 %own.1 = (f32[8,512,128]{2,1,0:T(8,128)}, f32[8,512,128]{2,1,0:T(8,128)}) custom-call(bf16[8,512,128]{2,1,0:T(8,128)(2,1)} %bitcast.10, bf16[64,136,128]{2,1,0:T(8,128)(2,1)} %get-tuple-element.19.kv_ref), custom_call_target="tpu_custom_call" | custom-call | flops 107374182400 | bytes 104857600 | tf_op jit(solution)/shard_map/own/pallas_call | solution.py:180
  42.3 0.0 copy-done.4
  42.3 12.6 %collective-permute-start.1 = (bf16[8,512,128]{2,1,0:T(8,128)(2,1)S(1)}, bf16[8,512,128]{2,1,0:T(8,128)(2,1)}, u32[]{:S(2)}, u32[]{:S(2)}) collective-permute-start(bf16[8,512,128]{2,1,0:T(8,128)(2,1)S(1)} %copy-done.4), channel_id=1, source_target_pairs={{0,8},{8,16},{16,24},{24,32},{32,40},{40,48},{48,56},{56,64},{64,7... | collective-permute-start | bytes 3145736 | tf_op jit(solution)/shard_map/ppermute | solution.py:192
  54.9 0.0 copy-done.3
  54.9 0.1 fusion.3
  55.0 0.1 copy.32
  55.1 0.6 reshape.38.flag_ref
  55.8 0.2 copy.29
  55.9 0.2 reshape.35.table_ref
  56.1 0.5 iota_compare_fusion
  56.6 84.2 %all-to-all-done.parts_ref = bf16[64,136,128]{2,1,0:T(8,128)(2,1)S(1)} async-done(((bf16[64,136,128]{2,1,0:T(8,128)(2,1)}), bf16[64,136,128]{2,1,0:T(8,128)(2,1)S(1)}, u32[]{:S(2)}, u32[]{:S(2)}) %all-to-all-start) | async-done | bytes 2228256 | tf_op jit(solution)/shard_map/all_to_all | solution.py:168
  140.8 2.9 pick.1
  143.7 0.0 copy-start
  143.7 2.0 copy-done
  145.7 8.5 %all-to-all-start.1 = ((bf16[64,256,128]{2,1,0:T(8,128)(2,1)}), bf16[64,256,128]{2,1,0:T(8,128)(2,1)}, u32[]{:S(2)}, u32[]{:S(2)}) async-start(bf16[64,256,128]{2,1,0:T(8,128)(2,1)} %copy-done), calls=%async_computation.1 | async-start | bytes 8388608 | tf_op jit(solution)/shard_map/all_to_all | solution.py:203
  154.2 0.0 collective-permute-done.1.v_ref
  154.2 0.0 copy-start.2
  154.2 0.0 copy-start.5
  154.2 17.2 %before.1 = (f32[8,512,128]{2,1,0:T(8,128)}, f32[8,512,128]{2,1,0:T(8,128)}) custom-call(s32[1]{0:T(128)} %bitcast.2.flag_ref, bf16[8,512,128]{2,1,0:T(8,128)(2,1)} %bitcast.11, bf16[8,512,128]{2,1,0:T(8,128)(2,1)} %collective-permute-done.k_ref, bf16[8,512,128]{2,1,0:T(8,128)(2,1)} %collective-permute-done.1.v_ref, ...), custom_call_target="tpu_custom_call" | custom-call | flops 429496729600 | bytes 419430400 | tf_op jit(solution)/shard_map/before/pallas_call | solution.py:210
  171.5 0.0 copy-done.2
  171.5 0.0 copy-done.5
  171.5 1.3 fusion.1
  172.8 169.5 %all-to-all-done.1.kv_ref = bf16[64,256,128]{2,1,0:T(8,128)(2,1)} async-done(((bf16[64,256,128]{2,1,0:T(8,128)(2,1)}), bf16[64,256,128]{2,1,0:T(8,128)(2,1)}, u32[]{:S(2)}, u32[]{:S(2)}) %all-to-all-start.1) | async-done | bytes 4194336 | tf_op jit(solution)/shard_map/all_to_all | solution.py:203
  342.3 10.9 %far.1 = bf16[8,512,128]{2,1,0:T(8,128)(2,1)} custom-call(s32[16]{0:T(128)} %reshape.38.flag_ref, bf16[8,512,128]{2,1,0:T(8,128)(2,1)} %bitcast.12, bf16[64,256,128]{2,1,0:T(8,128)(2,1)} %all-to-all-done.1.kv_ref, f32[8,512,128]{2,1,0:T(8,128)} %get-tuple-element.30.acc_ref, f32[8,512,128]{2,1,0:T(8,128)} %get-tuple-element.31.stat_ref), custom_call_target="tpu_custom_call" | custom-call | flops 2147483648 | bytes 10485760 | tf_op jit(solution)/shard_map/far/pallas_call | solution.py:228
  353.2 2.9 copy.31
  (7 shorter events, 0.0 us)
Async XLA Ops:
  5.5 27.7 %collective-permute-start = (bf16[8,512,128]{2,1,0:T(8,128)(2,1)}, bf16[8,512,128]{2,1,0:T(8,128)(2,1)}, u32[]{:S(2)}, u32[]{:S(2)}) collective-permute-start(bf16[8,512,128]{2,1,0:T(8,128)(2,1)} %get-tuple-element.17), channel_id=1, source_target_pairs={{0,8},{8,16},{16,24},{24,32},{32,40},{40,48},{48,56},{56,64},{64,7... | collective-permute-start | bytes 3145736 | tf_op jit(solution)/shard_map/ppermute | solution.py:167
  10.3 17.0 %copy-start.1 = (bf16[512,8,128]{2,1,0:T(8,128)(2,1)S(1)}, bf16[512,8,128]{2,1,0:T(8,128)(2,1)}, u32[]{:S(2)}) copy-start(bf16[512,8,128]{2,1,0:T(8,128)(2,1)} %param.4) | copy-start | bytes 3145732
  10.3 130.5 %all-to-all-start = ((bf16[64,136,128]{2,1,0:T(8,128)(2,1)}), bf16[64,136,128]{2,1,0:T(8,128)(2,1)S(1)}, u32[]{:S(2)}, u32[]{:S(2)}) async-start(bf16[64,136,128]{2,1,0:T(8,128)(2,1)} %get-tuple-element.19.kv_ref), calls=%async_computation | async-start | bytes 4456448 | tf_op jit(solution)/shard_map/all_to_all | solution.py:168
  33.2 9.2 %copy-start.4 = (bf16[8,512,128]{2,1,0:T(8,128)(2,1)S(1)}, bf16[8,512,128]{2,1,0:T(8,128)(2,1)}, u32[]{:S(2)}) copy-start(bf16[8,512,128]{2,1,0:T(8,128)(2,1)} %get-tuple-element.27) | copy-start | bytes 3145732
  33.2 21.7 %copy-start.3 = (s32[64,8,3]{0,1,2:T(8,128)S(1)}, s32[64,8,3]{0,1,2:T(8,128)}, u32[]{:S(2)}) copy-start(s32[64,8,3]{0,1,2:T(8,128)} %param.7) | copy-start | bytes 18436
  42.3 111.9 %collective-permute-start.1 = (bf16[8,512,128]{2,1,0:T(8,128)(2,1)S(1)}, bf16[8,512,128]{2,1,0:T(8,128)(2,1)}, u32[]{:S(2)}, u32[]{:S(2)}) collective-permute-start(bf16[8,512,128]{2,1,0:T(8,128)(2,1)S(1)} %copy-done.4), channel_id=1, source_target_pairs={{0,8},{8,16},{16,24},{24,32},{32,40},{40,48},{48,56},{56,64},{64,7... | collective-permute-start | bytes 3145736 | tf_op jit(solution)/shard_map/ppermute | solution.py:192
  143.7 2.0 copy-start
  145.7 196.6 %all-to-all-start.1 = ((bf16[64,256,128]{2,1,0:T(8,128)(2,1)}), bf16[64,256,128]{2,1,0:T(8,128)(2,1)}, u32[]{:S(2)}, u32[]{:S(2)}) async-start(bf16[64,256,128]{2,1,0:T(8,128)(2,1)} %copy-done), calls=%async_computation.1 | async-start | bytes 8388608 | tf_op jit(solution)/shard_map/all_to_all | solution.py:203
  154.2 17.2 %copy-start.2 = (bf16[512,8,128]{2,1,0:T(8,128)(2,1)S(1)}, bf16[512,8,128]{2,1,0:T(8,128)(2,1)}, u32[]{:S(2)}) copy-start(bf16[512,8,128]{2,1,0:T(8,128)(2,1)} %param.4) | copy-start | bytes 3145732
  154.2 17.2 %copy-start.5 = (pred[64]{0:T(512)(128)(4,1)S(1)}, pred[64]{0:T(512)(128)(4,1)}, u32[]{:S(2)}) copy-start(pred[64]{0:T(512)(128)(4,1)} %iota_compare_fusion) | copy-start | bytes 196

commit v3 on v2

--- a/solution.py
+++ b/solution.py
@@ -15,18 +15,22 @@
 BF16 = jnp.bfloat16
 
 
-def pack_kernel(k_ref, v_ref, out_ref, kt_ref, vt_ref):
+def pack_kernel(q_ref, k_ref, v_ref, out_ref, qt_ref, back_ref, ahead_ref):
     block_len, heads, head_dim = k_ref.shape
     half = block_len // ROWS
+    given = back_ref.shape[0]
 
     def one(p, total):
         here = pl.ds(p * ROWS, ROWS)
+        by_head = jnp.transpose(q_ref[here].astype(F32), (1, 0, 2)).astype(BF16)
+        qt_ref[:, here] = by_head
+        back_ref[:, here] = by_head[:given]
         keys = k_ref[here].astype(F32)
         by_head = jnp.transpose(keys, (1, 0, 2)).astype(BF16)
-        kt_ref[:, here] = by_head
+        ahead_ref[0, :, here] = by_head[given:]
         out_ref[p, : heads * ROWS] = by_head.reshape(heads * ROWS, head_dim)
         by_head = jnp.transpose(v_ref[here].astype(F32), (1, 0, 2)).astype(BF16)
-        vt_ref[:, here] = by_head
+        ahead_ref[1, :, here] = by_head[given:]
         out_ref[p + half, : heads * ROWS] = by_head.reshape(heads * ROWS, head_dim)
         return total + jnp.sum(keys, 0)
 
@@ -73,19 +77,47 @@
     stat_ref[0] = jnp.where(lane < stat_ref.shape[2] // 2, top, total)
 
 
-def before_kernel(scale, flag_ref, q_ref, k_ref, v_ref, acc_ref, stat_ref, acc_out, stat_out):
-    scores = lax.dot_general(q_ref[0], k_ref[0], ACROSS, preferred_element_type=F32)
-    scores = jnp.where(flag_ref[0] > 0, scores, MASKED)
+def give_kernel(scale, q_ref, kv_ref, out_ref, lse_ref):
+    keys, values = halves(kv_ref[...])
+    scores = lax.dot_general(q_ref[0], keys, ACROSS, preferred_element_type=F32)
+    top = jnp.max(scores, 1, keepdims=True) * scale
+    weights = jnp.exp2(scores * scale - top)
+    total = jnp.sum(weights, 1, keepdims=True)
+    acc = jnp.dot(weights.astype(BF16), values, preferred_element_type=F32)
+    out_ref[0] = (acc / total).astype(BF16)
+    lse_ref[0] = jnp.broadcast_to(top + jnp.log2(total), lse_ref.shape[1:])
+
+
+def before_kernel(
+    scale, given, flag_ref, q_ref, kv_ref, got_ref, lse_ref, acc_ref, stat_ref, acc_out, stat_out
+):
     half = stat_ref.shape[2] // 2
     top_before = stat_ref[0][:, :1]
-    top = jnp.maximum(jnp.max(scores, 1, keepdims=True) * scale, top_before)
-    weights = jnp.exp2(scores * scale - top)
-    shrink = jnp.exp2(top_before - top)
-    total = jnp.sum(weights, 1, keepdims=True) + stat_ref[0][:, half : half + 1] * shrink
-    acc = jnp.dot(weights.astype(BF16), v_ref[0], preferred_element_type=F32)
-    acc_out[0] = acc + acc_ref[0] * shrink
+    total_before = stat_ref[0][:, half : half + 1]
     lane = lax.broadcasted_iota(jnp.int32, stat_ref.shape[1:], 1)
-    stat_out[0] = jnp.where(lane < half, top, total)
+
+    @pl.when(pl.program_id(0) < given)
+    def _():
+        row = lse_ref[pl.ds(pl.program_id(0), 1)]
+        lse = jnp.broadcast_to(row, (stat_ref.shape[2], row.shape[1])).T
+        lse = jnp.where(flag_ref[0] > 0, lse, MASKED)
+        top = jnp.maximum(lse, top_before)
+        share = jnp.exp2(lse - top)
+        shrink = jnp.exp2(top_before - top)
+        acc_out[0] = got_ref[0].astype(F32) * share + acc_ref[0] * shrink
+        stat_out[0] = jnp.where(lane < half, top, total_before * shrink + share)
+
+    @pl.when(pl.program_id(0) >= given)
+    def _():
+        scores = lax.dot_general(q_ref[0], kv_ref[0, 0], ACROSS, preferred_element_type=F32)
+        scores = jnp.where(flag_ref[0] > 0, scores, MASKED)
+        top = jnp.maximum(jnp.max(scores, 1, keepdims=True) * scale, top_before)
+        weights = jnp.exp2(scores * scale - top)
+        shrink = jnp.exp2(top_before - top)
+        total = jnp.sum(weights, 1, keepdims=True) + total_before * shrink
+        acc = jnp.dot(weights.astype(BF16), kv_ref[1, 0], preferred_element_type=F32)
+        acc_out[0] = acc + acc_ref[0] * shrink
+        stat_out[0] = jnp.where(lane < half, top, total)
 
 
 def far_kernel(scale, flag_ref, q_ref, kv_ref, acc_ref, stat_ref, out_ref):
@@ -153,18 +185,23 @@
     pair = pl.BlockSpec((ctx_size, 2 * ROWS, head_dim), lambda h, *_: (0, h, 0))
     by_head = functools.partial(jax.ShapeDtypeStruct, (heads, block_len, head_dim))
 
-    send, keys, values = pl.pallas_call(
+    given = 5
+    send, q, queries_back, rows_ahead = pl.pallas_call(
         pack_kernel,
         out_shape=[
             jax.ShapeDtypeStruct((ctx_size, heads * (ROWS + 1), head_dim), BF16),
             by_head(BF16),
-            by_head(BF16),
+            jax.ShapeDtypeStruct((given, block_len, head_dim), BF16),
+            jax.ShapeDtypeStruct((2, heads - given, block_len, head_dim), BF16),
         ],
         compiler_params=params,
         name="pack",
-    )(key_rows, value_rows)
+    )(queries, key_rows, value_rows)
+    back = [(i + 1, i) for i in range(ctx_size - 1)]
     ahead = [(i, i + 1) for i in range(ctx_size - 1)]
-    keys_before = lax.ppermute(keys, "ctx", ahead)
+    next_queries = lax.ppermute(queries_back, "ctx", back)
+    rows_before = lax.ppermute(rows_ahead, "ctx", ahead)
+    next_queries, rows_before = lax.optimization_barrier((next_queries, rows_before))
     parts = lax.all_to_all(send, "ctx", split_axis=0, concat_axis=0, tiled=True)
 
     owner = jnp.arange(blocks, dtype=jnp.int32)[:, None]
@@ -175,21 +212,23 @@
     mine = lax.dynamic_index_in_dim(picks, position, 0, keepdims=False)
     usable = (mine < position).astype(jnp.int32).reshape(-1)
 
-    q = queries.transpose(1, 0, 2)
-    own_q, keys_before = lax.optimization_barrier((q, keys_before))
-    own = pl.pallas_call(
-        functools.partial(own_kernel, scale),
-        grid=(heads,),
+    gift, gift_lse = pl.pallas_call(
+        functools.partial(give_kernel, scale),
+        grid=(given,),
         in_specs=[whole, piece],
         out_specs=[whole, whole],
-        out_shape=[by_head(F32), by_head(F32)],
+        out_shape=[
+            jax.ShapeDtypeStruct((given, block_len, head_dim), BF16),
+            jax.ShapeDtypeStruct((given, block_len, head_dim), F32),
+        ],
         compiler_params=params,
         cost_estimate=cost(200, 200),
-        name="own",
-    )(own_q, send)
-    own, values = lax.optimization_barrier((own, values))
-    own, parts = lax.optimization_barrier((own, parts))
-    values_before = lax.ppermute(values, "ctx", ahead)
+        name="give",
+    )(next_queries, send)
+    gift_lse = gift_lse[:, :, 0]
+    got = lax.ppermute(gift, "ctx", ahead)
+    got_lse = lax.ppermute(gift_lse, "ctx", ahead)
+    parts, _ = lax.optimization_barrier((parts, gift_lse))
 
     picked = pl.pallas_call(
         pick_kernel,
@@ -207,10 +246,29 @@
     causal = jnp.arange(blocks, dtype=jnp.int32) <= position
     affinity = jnp.where(causal, per_head, 0.0).astype(BF16).transpose(1, 0, 2)
 
+    own = pl.pallas_call(
+        functools.partial(own_kernel, scale),
+        grid=(heads,),
+        in_specs=[whole, piece],
+        out_specs=[whole, whole],
+        out_shape=[by_head(F32), by_head(F32)],
+        compiler_params=params,
+        cost_estimate=cost(2, 12),
+        name="own",
+    )(q, send)
+    first = pl.BlockSpec(
+        (1, block_len, head_dim), lambda h, *_: (jnp.minimum(h, given - 1), 0, 0)
+    )
+    other = pl.BlockSpec(
+        (2, 1, block_len, head_dim), lambda h, *_: (0, jnp.maximum(h - given, 0), 0, 0)
+    )
     acc, stat = pl.pallas_call(
-        functools.partial(before_kernel, scale),
+        functools.partial(before_kernel, scale, given),
         grid_spec=pltpu.PrefetchScalarGridSpec(
-            num_scalar_prefetch=1, grid=(heads,), in_specs=[whole] * 5, out_specs=[whole, whole]
+            num_scalar_prefetch=1,
+            grid=(heads,),
+            in_specs=[whole, other, first, pl.BlockSpec((given, block_len), lambda h, *_: (0, 0)), whole, whole],
+            out_specs=[whole, whole],
         ),
         out_shape=[by_head(F32), by_head(F32)],
         compiler_params=params,
@@ -219,8 +277,9 @@
     )(
         (position > 0).astype(jnp.int32).reshape(1),
         q,
-        keys_before,
-        values_before,
+        rows_before,
+        got,
+        got_lse,
         *own,
     )
     group = 2

time: 357 us -> 351 us (0.983)
  waiting for transfers between devices: 258 us -> 249 us
    all_to_all x1, waiting for transfers between devices: 84.2 us -> 76.5 us  [body(): parts = lax.all_to_all(send, 'ctx', split_axis=0, concat_axis=0, tiled=True)]
    ppermute x2 -> x4, starting transfers between devices: 17.4 us -> 12 us  [the longest x1 3.86 us: body(): rows_before = lax.ppermute(rows_ahead, 'ctx', ahead)]
    ppermute x2 -> x4, waiting for transfers between devices: 4.71 us -> 0.01 us  [the longest x1 0.01 us: body(): next_queries = lax.ppermute(queries_back, 'ctx', back)]
    all_to_all x1, starting transfers between devices: 17 us -> 20.6 us  [body(): parts = lax.all_to_all(send, 'ctx', split_axis=0, concat_axis=0, tiled=True)]
    pallas_call x1 -> x2, Pallas kernels: 17.2 us -> 18.6 us  [the longest x1 12.1 us: body(): pl.pallas_call(functools.partial(before_kernel, scale, given), grid_spec=...]
  transfers between devices with their start and end apart: 4 -> 6, of which waited for: 3 -> 2; matrix products, arithmetic and copies ran while one was open for 1% -> 2% of each run, Pallas kernels for 8% -> 9%
where the time goes in v3:
time: 351 us; the launch traced here: 350 us
  waiting for transfers between devices  249 us (71%)
  Pallas kernels  47.2 us (13%)
  starting transfers between devices  41.4 us (12%)
  local copies, waits for them, and re-layouts  10.4 us (3%)
    all_to_all x1, waiting for transfers between devices, body(): lax.all_to_all(picked, 'ctx', split_axis=0, concat_axis=0, tiled=True)  172 us
    all_to_all x1, waiting for transfers between devices, body(): parts = lax.all_to_all(send, 'ctx', split_axis=0, concat_axis=0, tiled=True)  76.5 us
    all_to_all x1, starting transfers between devices, body(): parts = lax.all_to_all(send, 'ctx', split_axis=0, concat_axis=0, tiled=True)  20.6 us
    pallas_call x1, Pallas kernels, body(): pl.pallas_call(functools.partial(before_kernel, scale, given), grid_spec=...  12.1 us
    pallas_call x1, Pallas kernels, body(): pl.pallas_call(functools.partial(far_kernel, scale), grid_spec=pltpu.Pref...  10.9 us
    pallas_call x1, Pallas kernels, body(): pl.pallas_call(functools.partial(own_kernel, scale), grid=(heads,), in_sp...  9.08 us
    all_to_all x1, starting transfers between devices, body(): lax.all_to_all(picked, 'ctx', split_axis=0, concat_axis=0, tiled=True)  8.83 us
  transfers between devices with their start and end apart: 6, of which 2 were waited for; matrix products, arithmetic and copies ran while one was open for 2% of the time, Pallas kernels for 9%

profile of v3, /device:TPU:6, one launch (start us, length us, event | category | flops | bytes accessed | tf_op | source)
XLA Modules:
  0.0 350.5 jit_solution(7788393365253048684)
XLA Ops:
  0.6 5.7 %pack.1 = (bf16[64,136,128]{2,1,0:T(8,128)(2,1)}, bf16[8,512,128]{2,1,0:T(8,128)(2,1)}, bf16[5,512,128]{2,1,0:T(8,128)(2,1)}, bf16[2,3,512,128]{3,2,1,0:T(8,128)(2,1)}) custom-call(bf16[512,8,128]{2,1,0:T(8,128)(2,1)} %q_ref.1, bf16[512,8,128]{2,1,0:T(8,128)(2,1)} %k_ref.1, bf16[512,8,128]{2,1,0:T(8,128)(2,1)} %v_ref.1), custom_call_target="tpu_custom_call" | custom-call | tf_op jit(solution)/shard_map/pack/pallas_call | solution.py:189
  6.3 3.9 %collective-permute-start.1 = (bf16[2,3,512,128]{3,2,1,0:T(8,128)(2,1)}, bf16[2,3,512,128]{3,2,1,0:T(8,128)(2,1)S(1)}, u32[]{:S(2)}, u32[]{:S(2)}) collective-permute-start(bf16[2,3,512,128]{3,2,1,0:T(8,128)(2,1)} %get-tuple-element.18), channel_id=1, source_target_pairs={{0,8},{8,16},{16,24},{24,32},{32,40},{40,48},{48,56},{56,64},{64,7... | collective-permute-start | bytes 2359304 | tf_op jit(solution)/shard_map/ppermute | solution.py:203
  10.2 1.3 collective-permute-start
  11.5 0.0 copy-start.2
  11.5 20.6 %all-to-all-start = ((bf16[64,136,128]{2,1,0:T(8,128)(2,1)}), bf16[64,136,128]{2,1,0:T(8,128)(2,1)S(1)}, u32[]{:S(2)}, u32[]{:S(2)}) async-start(bf16[64,136,128]{2,1,0:T(8,128)(2,1)} %get-tuple-element.16.kv_ref), calls=%async_computation | async-start | bytes 4456448 | tf_op jit(solution)/shard_map/all_to_all | solution.py:205
  32.2 0.1 fusion.3
  32.3 0.1 copy.32
  32.4 0.0 collective-permute-done.q_ref
  32.4 0.0 collective-permute-done.1.kv_ref
  32.4 6.5 %give.1 = (bf16[5,512,128]{2,1,0:T(8,128)(2,1)}, f32[5,512,128]{2,1,0:T(8,128)}) custom-call(bf16[5,512,128]{2,1,0:T(8,128)(2,1)} %collective-permute-done.q_ref, bf16[64,136,128]{2,1,0:T(8,128)(2,1)} %get-tuple-element.16.kv_ref), custom_call_target="tpu_custom_call" | custom-call | flops 107374182400 | bytes 104857600 | tf_op jit(solution)/shard_map/give/pallas_call | solution.py:215
  39.0 3.5 collective-permute-start.2
  42.5 0.5 iota_compare_fusion
  43.0 2.9 copy.29
  45.9 0.7 slice_bitcast_fusion
  46.7 3.3 collective-permute-start.3
  50.0 9.1 %own.1 = (f32[8,512,128]{2,1,0:T(8,128)}, f32[8,512,128]{2,1,0:T(8,128)}) custom-call(bf16[8,512,128]{2,1,0:T(8,128)(2,1)} %get-tuple-element.15.q_ref, bf16[64,136,128]{2,1,0:T(8,128)(2,1)} %get-tuple-element.16.kv_ref), custom_call_target="tpu_custom_call" | custom-call | flops 1073741824 | bytes 6291456 | tf_op jit(solution)/shard_map/own/pallas_call | solution.py:249
  59.1 0.6 reshape.38.flag_ref
  59.7 0.1 copy.28
  59.8 0.2 reshape.35.table_ref
  60.0 76.5 %all-to-all-done.parts_ref = bf16[64,136,128]{2,1,0:T(8,128)(2,1)S(1)} async-done(((bf16[64,136,128]{2,1,0:T(8,128)(2,1)}), bf16[64,136,128]{2,1,0:T(8,128)(2,1)S(1)}, u32[]{:S(2)}, u32[]{:S(2)}) %all-to-all-start) | async-done | bytes 2228256 | tf_op jit(solution)/shard_map/all_to_all | solution.py:205
  136.5 2.9 pick.1
  139.4 2.0 copy-done
  141.4 8.8 %all-to-all-start.1 = ((bf16[64,256,128]{2,1,0:T(8,128)(2,1)}), bf16[64,256,128]{2,1,0:T(8,128)(2,1)}, u32[]{:S(2)}, u32[]{:S(2)}) async-start(bf16[64,256,128]{2,1,0:T(8,128)(2,1)} %copy-done), calls=%async_computation.1 | async-start | bytes 8388608 | tf_op jit(solution)/shard_map/all_to_all | solution.py:242
  150.2 0.0 collective-permute-done.3.lse_ref
  150.2 0.0 copy-start.5
  150.2 0.0 collective-permute-done.2.got_ref
  150.3 0.9 copy-done.4
  151.1 12.1 %before.1 = (f32[8,512,128]{2,1,0:T(8,128)}, f32[8,512,128]{2,1,0:T(8,128)}) custom-call(s32[1]{0:T(128)} %bitcast.2.flag_ref, bf16[8,512,128]{2,1,0:T(8,128)(2,1)} %get-tuple-element.15.q_ref, bf16[2,3,512,128]{3,2,1,0:T(8,128)(2,1)} %copy-done.3, bf16[5,512,128]{2,1,0:T(8,128)(2,1)} %copy-done.4, f32[5,512]{1,0:T(8,128)} %copy-done.5, ...), custom_call_target="tpu_custom_call" | custom-call | flops 429496729600 | bytes 419430400 | tf_op jit(solution)/shard_map/before/pallas_call | solution.py:265
  163.3 1.3 fusion.1
  164.5 172.2 %all-to-all-done.1.kv_ref = bf16[64,256,128]{2,1,0:T(8,128)(2,1)} async-done(((bf16[64,256,128]{2,1,0:T(8,128)(2,1)}), bf16[64,256,128]{2,1,0:T(8,128)(2,1)}, u32[]{:S(2)}, u32[]{:S(2)}) %all-to-all-start.1) | async-done | bytes 4194336 | tf_op jit(solution)/shard_map/all_to_all | solution.py:242
  336.7 10.9 %far.1 = bf16[8,512,128]{2,1,0:T(8,128)(2,1)} custom-call(s32[16]{0:T(128)} %reshape.38.flag_ref, bf16[8,512,128]{2,1,0:T(8,128)(2,1)} %get-tuple-element.15.q_ref, bf16[64,256,128]{2,1,0:T(8,128)(2,1)} %all-to-all-done.1.kv_ref, f32[8,512,128]{2,1,0:T(8,128)} %get-tuple-element.26.acc_ref, f32[8,512,128]{2,1,0:T(8,128)} %get-tuple-element.27.stat_ref), custom_call_target="tpu_custom_call" | custom-call | flops 2147483648 | bytes 10485760 | tf_op jit(solution)/shard_map/far/pallas_call | solution.py:287
  347.6 2.9 copy.31
  (15 shorter events, 0.0 us)
Async XLA Ops:
  6.3 26.1 %collective-permute-start.1 = (bf16[2,3,512,128]{3,2,1,0:T(8,128)(2,1)}, bf16[2,3,512,128]{3,2,1,0:T(8,128)(2,1)S(1)}, u32[]{:S(2)}, u32[]{:S(2)}) collective-permute-start(bf16[2,3,512,128]{3,2,1,0:T(8,128)(2,1)} %get-tuple-element.18), channel_id=1, source_target_pairs={{0,8},{8,16},{16,24},{24,32},{32,40},{40,48},{48,56},{56,64},{64,7... | collective-permute-start | bytes 2359304 | tf_op jit(solution)/shard_map/ppermute | solution.py:203
  10.2 22.2 %collective-permute-start = (bf16[5,512,128]{2,1,0:T(8,128)(2,1)}, bf16[5,512,128]{2,1,0:T(8,128)(2,1)}, u32[]{:S(2)}, u32[]{:S(2)}) collective-permute-start(bf16[5,512,128]{2,1,0:T(8,128)(2,1)} %get-tuple-element.17), channel_id=1, source_target_pairs={{8,0},{16,8},{24,16},{32,24},{40,32},{48,40},{56,48},{64,56},{72,6... | collective-permute-start | bytes 1966088 | tf_op jit(solution)/shard_map/ppermute | solution.py:202
  11.5 20.7 %copy-start.2 = (s32[64,8,3]{0,1,2:T(8,128)S(1)}, s32[64,8,3]{0,1,2:T(8,128)}, u32[]{:S(2)}) copy-start(s32[64,8,3]{0,1,2:T(8,128)} %param.7) | copy-start | bytes 18436
  11.5 125.0 %all-to-all-start = ((bf16[64,136,128]{2,1,0:T(8,128)(2,1)}), bf16[64,136,128]{2,1,0:T(8,128)(2,1)S(1)}, u32[]{:S(2)}, u32[]{:S(2)}) async-start(bf16[64,136,128]{2,1,0:T(8,128)(2,1)} %get-tuple-element.16.kv_ref), calls=%async_computation | async-start | bytes 4456448 | tf_op jit(solution)/shard_map/all_to_all | solution.py:205
  32.4 6.5 %copy-start.3 = (bf16[2,3,512,128]{3,2,1,0:T(8,128)(2,1)}, bf16[2,3,512,128]{3,2,1,0:T(8,128)(2,1)S(1)}, u32[]{:S(2)}) copy-start(bf16[2,3,512,128]{3,2,1,0:T(8,128)(2,1)S(1)} %collective-permute-done.1.kv_ref) | copy-start | bytes 2359300
  39.0 111.3 %collective-permute-start.2 = (bf16[5,512,128]{2,1,0:T(8,128)(2,1)}, bf16[5,512,128]{2,1,0:T(8,128)(2,1)S(1)}, u32[]{:S(2)}, u32[]{:S(2)}) collective-permute-start(bf16[5,512,128]{2,1,0:T(8,128)(2,1)} %get-tuple-element.23), channel_id=1, source_target_pairs={{0,8},{8,16},{16,24},{24,32},{32,40},{40,48},{48,56},{56,64},{64,7... | collective-permute-start | bytes 1966088 | tf_op jit(solution)/shard_map/ppermute | solution.py:229
  46.7 103.6 %collective-permute-start.3 = (f32[5,512]{1,0:T(8,128)S(1)}, f32[5,512]{1,0:T(8,128)S(1)}, u32[]{:S(2)}, u32[]{:S(2)}) collective-permute-start(f32[5,512]{1,0:T(8,128)S(1)} %slice_bitcast_fusion), channel_id=1, source_target_pairs={{0,8},{8,16},{16,24},{24,32},{32,40},{40,48},{48,56},{56,64},{64,7... | collective-permute-start | bytes 30728 | tf_op jit(solution)/shard_map/ppermute | solution.py:230
  139.4 2.0 copy-start
  141.4 195.3 %all-to-all-start.1 = ((bf16[64,256,128]{2,1,0:T(8,128)(2,1)}), bf16[64,256,128]{2,1,0:T(8,128)(2,1)}, u32[]{:S(2)}, u32[]{:S(2)}) async-start(bf16[64,256,128]{2,1,0:T(8,128)(2,1)} %copy-done), calls=%async_computation.1 | async-start | bytes 8388608 | tf_op jit(solution)/shard_map/all_to_all | solution.py:242
  150.2 0.9 copy-start.5
  150.2 0.9 copy-start.4
  151.1 12.1 %copy-start.1 = (bf16[8,512,128]{2,1,0:T(8,128)(2,1)S(1)}, bf16[8,512,128]{2,1,0:T(8,128)(2,1)}, u32[]{:S(2)}) copy-start(bf16[8,512,128]{2,1,0:T(8,128)(2,1)} %get-tuple-element.15.q_ref) | copy-start | bytes 3145732
  151.1 12.1 %copy-start.6 = (pred[64]{0:T(512)(128)(4,1)S(1)}, pred[64]{0:T(512)(128)(4,1)}, u32[]{:S(2)}) copy-start(pred[64]{0:T(512)(128)(4,1)} %iota_compare_fusion) | copy-start | bytes 196

commit v4 on v3

--- a/solution.py
+++ b/solution.py
@@ -15,33 +15,46 @@
 BF16 = jnp.bfloat16
 
 
-def pack_kernel(q_ref, k_ref, v_ref, out_ref, qt_ref, back_ref, ahead_ref):
-    block_len, heads, head_dim = k_ref.shape
-    half = block_len // ROWS
+def pack_kernel(q_ref, k_ref, v_ref, out_ref, qt_ref, back_ref, ahead_ref, total_ref):
+    tokens, heads, head_dim = k_ref.shape
+    count = tokens // ROWS
+    step, steps = pl.program_id(0), pl.num_programs(0)
+    half = count * steps
     given = back_ref.shape[0]
+
+    @pl.when(step == 0)
+    def _():
+        total_ref[...] = jnp.zeros_like(total_ref)
 
     def one(p, total):
         here = pl.ds(p * ROWS, ROWS)
+        slot = step * count + p
         by_head = jnp.transpose(q_ref[here].astype(F32), (1, 0, 2)).astype(BF16)
         qt_ref[:, here] = by_head
         back_ref[:, here] = by_head[:given]
         keys = k_ref[here].astype(F32)
         by_head = jnp.transpose(keys, (1, 0, 2)).astype(BF16)
         ahead_ref[0, :, here] = by_head[given:]
-        out_ref[p, : heads * ROWS] = by_head.reshape(heads * ROWS, head_dim)
+        out_ref[slot, : heads * ROWS] = by_head.reshape(heads * ROWS, head_dim)
         by_head = jnp.transpose(v_ref[here].astype(F32), (1, 0, 2)).astype(BF16)
         ahead_ref[1, :, here] = by_head[given:]
-        out_ref[p + half, : heads * ROWS] = by_head.reshape(heads * ROWS, head_dim)
+        out_ref[slot + half, : heads * ROWS] = by_head.reshape(heads * ROWS, head_dim)
         return total + jnp.sum(keys, 0)
 
-    total = lax.fori_loop(0, half, one, jnp.zeros((heads, head_dim), F32), unroll=4)
-    pooled = (total / block_len).astype(BF16)
-
-    def spread(p, carry):
-        out_ref[p, heads * ROWS :] = pooled
-        return carry
-
-    lax.fori_loop(0, 2 * half, spread, 0, unroll=8)
+    total = total_ref[...]
+    for p in range(count):
+        total = one(p, total)
+    total_ref[...] = total
+
+    @pl.when(step == steps - 1)
+    def _():
+        pooled = (total / (tokens * steps)).astype(BF16)
+
+        def spread(p, carry):
+            out_ref[p, heads * ROWS :] = pooled
+            return carry
+
+        lax.fori_loop(0, 2 * half, spread, 0, unroll=8)
 
 
 def pick_kernel(table_ref, parts_ref, out_ref):
@@ -89,12 +102,16 @@
 
 
 def before_kernel(
-    scale, given, flag_ref, q_ref, kv_ref, got_ref, lse_ref, acc_ref, stat_ref, acc_out, stat_out
+    scale, given, flag_ref, q_ref, kv_ref, got_ref, lse_ref, acc_ref, stat_ref, acc_out, lse_out
 ):
     half = stat_ref.shape[2] // 2
     top_before = stat_ref[0][:, :1]
     total_before = stat_ref[0][:, half : half + 1]
-    lane = lax.broadcasted_iota(jnp.int32, stat_ref.shape[1:], 1)
+
+    def put(acc, top, total):
+        acc_out[0] = acc / total
+        lse = jnp.broadcast_to(top + jnp.log2(total), stat_ref.shape[1:])
+        lse_out[0] = lse.T[:1]
 
     @pl.when(pl.program_id(0) < given)
     def _():
@@ -104,8 +121,8 @@
         top = jnp.maximum(lse, top_before)
         share = jnp.exp2(lse - top)
         shrink = jnp.exp2(top_before - top)
-        acc_out[0] = got_ref[0].astype(F32) * share + acc_ref[0] * shrink
-        stat_out[0] = jnp.where(lane < half, top, total_before * shrink + share)
+        acc = got_ref[0].astype(F32) * share + acc_ref[0] * shrink
+        put(acc, top, total_before * shrink + share)
 
     @pl.when(pl.program_id(0) >= given)
     def _():
@@ -116,51 +133,40 @@
         shrink = jnp.exp2(top_before - top)
         total = jnp.sum(weights, 1, keepdims=True) + total_before * shrink
         acc = jnp.dot(weights.astype(BF16), kv_ref[1, 0], preferred_element_type=F32)
-        acc_out[0] = acc + acc_ref[0] * shrink
-        stat_out[0] = jnp.where(lane < half, top, total)
-
-
-def far_kernel(scale, flag_ref, q_ref, kv_ref, acc_ref, stat_ref, out_ref):
-    group, block_len, head_dim = q_ref.shape
-    half = stat_ref.shape[2] // 2
-    first_head = pl.program_id(0) * group
-    step = block_len // 2
-    heads = []
-    for h in range(group):
-        both = [halves(kv_ref[:, (2 * h + s) * ROWS : (2 * h + s + 1) * ROWS]) for s in range(2)]
-        keys = jnp.concatenate([both[0][0], both[1][0]], 0)
-        values = jnp.concatenate([both[0][1], both[1][1]], 0)
+        put(acc + acc_ref[0] * shrink, top, total)
+
+
+def far_kernel(scale, flag_ref, q_ref, kv_ref, acc_ref, lse_ref, out_ref):
+    count, step, head_dim = q_ref.shape
+
+    def score(h):
+        keys = jnp.concatenate(
+            [halves(kv_ref[:, (2 * h + s) * ROWS : (2 * h + s + 1) * ROWS])[0] for s in range(2)], 0
+        )
+        off = [jnp.where(flag_ref[2 * h + s] > 0, 0.0, MASKED) for s in range(2)]
+        col = lax.broadcasted_iota(jnp.int32, (1, keys.shape[0]), 1)
+        scores = lax.dot_general(q_ref[h], keys, ACROSS, preferred_element_type=F32)
+        return scores + jnp.where(col < keys.shape[0] // 2, off[0], off[1])
+
+    def finish(h, scores):
+        values = jnp.concatenate(
+            [halves(kv_ref[:, (2 * h + s) * ROWS : (2 * h + s + 1) * ROWS])[1] for s in range(2)], 0
+        )
         values = jnp.concatenate([values, jnp.ones_like(values)], 1)
-        off = [
-            jnp.where(flag_ref[2 * (first_head + h) + s] > 0, 0.0, MASKED) for s in range(2)
-        ]
-        col = lax.broadcasted_iota(jnp.int32, (1, keys.shape[0]), 1)
-        heads.append((keys, values, jnp.where(col < block_len, off[0], off[1])))
-
-    def score(h, start):
-        keys, _, off = heads[h]
-        q = q_ref[h, start : start + step]
-        return lax.dot_general(q, keys, ACROSS, preferred_element_type=F32) + off
-
-    def finish(h, start, scores):
-        _, values, _ = heads[h]
-        here = pl.ds(start, step)
-        stat = stat_ref[h, here]
-        top_before = stat[:, :1]
-        top = jnp.maximum(jnp.max(scores, 1, keepdims=True) * scale, top_before)
-        weights = jnp.exp2(scores * scale - top).astype(BF16)
-        shrink = jnp.exp2(top_before - top)
+        lse = jnp.broadcast_to(lse_ref[h : h + 1], (head_dim, step)).T
+        top = jnp.maximum(jnp.max(scores, 1, keepdims=True) * scale, lse)
+        weights = jnp.exp2(scores * scale - top[:, :1]).astype(BF16)
+        share = jnp.exp2(lse - top)
         both = jnp.dot(weights, values, preferred_element_type=F32)
-        acc = acc_ref[h, here] * shrink + both[:, :head_dim]
-        total = stat[:, half : half + 1] * shrink + both[:, head_dim:]
-        out_ref[h, here] = (acc / total).astype(BF16)
-
-    todo = [(h, start) for h in range(group) for start in range(0, block_len, step)]
-    scores = score(*todo[0])
-    for index, item in enumerate(todo):
-        following = score(*todo[index + 1]) if index + 1 < len(todo) else None
-        finish(*item, scores)
+        return (acc_ref[h] * share + both[:, :head_dim]) / (share + both[:, head_dim:])
+
+    results = []
+    scores = score(0)
+    for h in range(count):
+        following = score(h + 1) if h + 1 < count else None
+        results.append(finish(h, scores))
         scores = following
+    out_ref[...] = jnp.transpose(jnp.stack(results, 0), (1, 0, 2)).astype(BF16)
 
 
 def body(queries, key_rows, value_rows, selection):
@@ -186,8 +192,19 @@
     by_head = functools.partial(jax.ShapeDtypeStruct, (heads, block_len, head_dim))
 
     given = 5
+    chunks = 4
+    tokens = block_len // chunks
     send, q, queries_back, rows_ahead = pl.pallas_call(
         pack_kernel,
+        grid=(chunks,),
+        in_specs=[pl.BlockSpec((tokens, heads, head_dim), lambda i: (i, 0, 0))] * 3,
+        out_specs=[
+            pl.BlockSpec((ctx_size, heads * (ROWS + 1), head_dim), lambda i: (0, 0, 0)),
+            pl.BlockSpec((heads, tokens, head_dim), lambda i: (0, i, 0)),
+            pl.BlockSpec((given, tokens, head_dim), lambda i: (0, i, 0)),
+            pl.BlockSpec((2, heads - given, tokens, head_dim), lambda i: (0, 0, i, 0)),
+        ],
+        scratch_shapes=[pltpu.VMEM((heads, head_dim), F32)],
         out_shape=[
             jax.ShapeDtypeStruct((ctx_size, heads * (ROWS + 1), head_dim), BF16),
             by_head(BF16),
@@ -262,15 +279,15 @@
     other = pl.BlockSpec(
         (2, 1, block_len, head_dim), lambda h, *_: (0, jnp.maximum(h - given, 0), 0, 0)
     )
-    acc, stat = pl.pallas_call(
+    acc, lse = pl.pallas_call(
         functools.partial(before_kernel, scale, given),
         grid_spec=pltpu.PrefetchScalarGridSpec(
             num_scalar_prefetch=1,
             grid=(heads,),
             in_specs=[whole, other, first, pl.BlockSpec((given, block_len), lambda h, *_: (0, 0)), whole, whole],
-            out_specs=[whole, whole],
+            out_specs=[whole, pl.BlockSpec((1, 1, block_len), lambda h, *_: (h, 0, 0))],
         ),
-        out_shape=[by_head(F32), by_head(F32)],
+        out_shape=[by_head(F32), jax.ShapeDtypeStruct((heads, 1, block_len), F32)],
         compiler_params=params,
         cost_estimate=cost(800, 800),
         name="before",
@@ -282,27 +299,27 @@
         got_lse,
         *own,
     )
-    group = 2
-    some = pl.BlockSpec((group, block_len, head_dim), lambda h, *_: (h, 0, 0))
-    out = pl.pallas_call(
+    step = block_len // 2
+    some = pl.BlockSpec((heads, step, head_dim), lambda i, *_: (0, i, 0))
+    attended = pl.pallas_call(
         functools.partial(far_kernel, scale),
         grid_spec=pltpu.PrefetchScalarGridSpec(
             num_scalar_prefetch=1,
-            grid=(heads // group,),
+            grid=(block_len // step,),
             in_specs=[
                 some,
-                pl.BlockSpec((ctx_size, group * 2 * ROWS, head_dim), lambda h, *_: (0, h, 0)),
+                pl.BlockSpec((ctx_size, heads * 2 * ROWS, head_dim), lambda i, *_: (0, 0, 0)),
                 some,
-                some,
+                pl.BlockSpec((heads, step), lambda i, *_: (0, i)),
             ],
-            out_specs=some,
+            out_specs=pl.BlockSpec((step, heads, head_dim), lambda i, *_: (i, 0, 0)),
         ),
-        out_shape=by_head(BF16),
+        out_shape=jax.ShapeDtypeStruct((block_len, heads, head_dim), BF16),
         compiler_params=params,
         cost_estimate=cost(4, 20),
         name="far",
-    )(usable, q, fetched, acc, stat)
-    return out.transpose(1, 0, 2), affinity
+    )(usable, q, fetched, acc, lse[:, 0])
+    return attended, affinity
 
 
 def solution(mesh):

time: 351 us -> 348 us (level)
  no operation moved by 1% of the time
where the time goes in v4:
time: 348 us; the launch traced here: 347 us
  waiting for transfers between devices  247 us (71%)
  Pallas kernels  47.3 us (14%)
  starting transfers between devices  41.4 us (12%)
  local copies, waits for them, and re-layouts  8.9 us (3%)
    all_to_all x1, waiting for transfers between devices, body(): lax.all_to_all(picked, 'ctx', split_axis=0, concat_axis=0, tiled=True)  170 us
    all_to_all x1, waiting for transfers between devices, body(): parts = lax.all_to_all(send, 'ctx', split_axis=0, concat_axis=0, tiled=True)  76.4 us
    all_to_all x1, starting transfers between devices, body(): parts = lax.all_to_all(send, 'ctx', split_axis=0, concat_axis=0, tiled=True)  20.6 us
    pallas_call x1, Pallas kernels, body(): pl.pallas_call(functools.partial(before_kernel, scale, given), grid_spec=...  12.6 us
    pallas_call x1, Pallas kernels, body(): pl.pallas_call(functools.partial(far_kernel, scale), grid_spec=pltpu.Pref...  10.7 us
    pallas_call x1, Pallas kernels, body(): pl.pallas_call(functools.partial(own_kernel, scale), grid=(heads,), in_sp...  9.08 us
    all_to_all x1, starting transfers between devices, body(): lax.all_to_all(picked, 'ctx', split_axis=0, concat_axis=0, tiled=True)  8.83 us
  transfers between devices with their start and end apart: 6, of which 2 were waited for; matrix products, arithmetic and copies ran while one was open for 2% of the time, Pallas kernels for 9%

profile of v4, /device:TPU:6, one launch (start us, length us, event | category | flops | bytes accessed | tf_op | source)
XLA Modules:
  0.0 347.1 jit_solution(15847363161330228982)
XLA Ops:
  0.6 5.4 %pack.1 = (bf16[64,136,128]{2,1,0:T(8,128)(2,1)}, bf16[8,512,128]{2,1,0:T(8,128)(2,1)}, bf16[5,512,128]{2,1,0:T(8,128)(2,1)}, bf16[2,3,512,128]{3,2,1,0:T(8,128)(2,1)}) custom-call(bf16[512,8,128]{2,1,0:T(8,128)(2,1)} %q_ref.1, bf16[512,8,128]{2,1,0:T(8,128)(2,1)} %k_ref.1, bf16[512,8,128]{2,1,0:T(8,128)(2,1)} %v_ref.1), custom_call_target="tpu_custom_call" | custom-call | tf_op jit(solution)/shard_map/pack/pallas_call | solution.py:197
  6.1 3.9 %collective-permute-start.1 = (bf16[2,3,512,128]{3,2,1,0:T(8,128)(2,1)}, bf16[2,3,512,128]{3,2,1,0:T(8,128)(2,1)S(1)}, u32[]{:S(2)}, u32[]{:S(2)}) collective-permute-start(bf16[2,3,512,128]{3,2,1,0:T(8,128)(2,1)} %get-tuple-element.18), channel_id=1, source_target_pairs={{0,8},{8,16},{16,24},{24,32},{32,40},{40,48},{48,56},{56,64},{64,7... | collective-permute-start | bytes 2359304 | tf_op jit(solution)/shard_map/ppermute | solution.py:220
  9.9 1.3 collective-permute-start
  11.2 0.0 copy-start.2
  11.3 20.6 %all-to-all-start = ((bf16[64,136,128]{2,1,0:T(8,128)(2,1)}), bf16[64,136,128]{2,1,0:T(8,128)(2,1)S(1)}, u32[]{:S(2)}, u32[]{:S(2)}) async-start(bf16[64,136,128]{2,1,0:T(8,128)(2,1)} %get-tuple-element.16.kv_ref), calls=%async_computation | async-start | bytes 4456448 | tf_op jit(solution)/shard_map/all_to_all | solution.py:222
  31.9 0.1 fusion.3
  32.0 0.1 copy.29
  32.2 0.0 collective-permute-done.q_ref
  32.2 0.0 collective-permute-done.1.kv_ref
  32.2 0.0 copy-start.3
  32.2 6.5 %give.1 = (bf16[5,512,128]{2,1,0:T(8,128)(2,1)}, f32[5,512,128]{2,1,0:T(8,128)}) custom-call(bf16[5,512,128]{2,1,0:T(8,128)(2,1)} %collective-permute-done.q_ref, bf16[64,136,128]{2,1,0:T(8,128)(2,1)} %get-tuple-element.16.kv_ref), custom_call_target="tpu_custom_call" | custom-call | flops 107374182400 | bytes 104857600 | tf_op jit(solution)/shard_map/give/pallas_call | solution.py:232
  38.7 3.5 %collective-permute-start.2 = (bf16[5,512,128]{2,1,0:T(8,128)(2,1)}, bf16[5,512,128]{2,1,0:T(8,128)(2,1)S(1)}, u32[]{:S(2)}, u32[]{:S(2)}) collective-permute-start(bf16[5,512,128]{2,1,0:T(8,128)(2,1)} %get-tuple-element.23), channel_id=1, source_target_pairs={{0,8},{8,16},{16,24},{24,32},{32,40},{40,48},{48,56},{56,64},{64,7... | collective-permute-start | bytes 1966088 | tf_op jit(solution)/shard_map/ppermute | solution.py:246
  42.2 0.6 iota_compare_fusion
  42.8 2.9 copy.26
  45.8 0.7 slice_bitcast_fusion
  46.5 3.3 collective-permute-start.3
  49.8 9.1 %own.1 = (f32[8,512,128]{2,1,0:T(8,128)}, f32[8,512,128]{2,1,0:T(8,128)}) custom-call(bf16[8,512,128]{2,1,0:T(8,128)(2,1)} %get-tuple-element.15.q_ref, bf16[64,136,128]{2,1,0:T(8,128)(2,1)} %get-tuple-element.16.kv_ref), custom_call_target="tpu_custom_call" | custom-call | flops 1073741824 | bytes 6291456 | tf_op jit(solution)/shard_map/own/pallas_call | solution.py:266
  58.9 0.6 reshape.38.flag_ref
  59.5 0.1 copy.25
  59.7 0.2 reshape.35.table_ref
  59.8 76.4 %all-to-all-done.parts_ref = bf16[64,136,128]{2,1,0:T(8,128)(2,1)S(1)} async-done(((bf16[64,136,128]{2,1,0:T(8,128)(2,1)}), bf16[64,136,128]{2,1,0:T(8,128)(2,1)S(1)}, u32[]{:S(2)}, u32[]{:S(2)}) %all-to-all-start) | async-done | bytes 2228256 | tf_op jit(solution)/shard_map/all_to_all | solution.py:222
  136.2 2.9 pick.1
  139.2 2.0 copy-done
  141.1 8.8 %all-to-all-start.1 = ((bf16[64,256,128]{2,1,0:T(8,128)(2,1)}), bf16[64,256,128]{2,1,0:T(8,128)(2,1)}, u32[]{:S(2)}, u32[]{:S(2)}) async-start(bf16[64,256,128]{2,1,0:T(8,128)(2,1)} %copy-done), calls=%async_computation.1 | async-start | bytes 8388608 | tf_op jit(solution)/shard_map/all_to_all | solution.py:259
  150.0 0.0 copy-start.5
  150.0 0.0 collective-permute-done.2.got_ref
  150.0 0.9 copy-done.4
  150.9 12.6 %before.1 = (f32[8,512,128]{2,1,0:T(8,128)}, f32[8,1,512]{2,1,0:T(1,128)}) custom-call(s32[1]{0:T(128)} %bitcast.2.flag_ref, bf16[8,512,128]{2,1,0:T(8,128)(2,1)} %get-tuple-element.15.q_ref, bf16[2,3,512,128]{3,2,1,0:T(8,128)(2,1)} %copy-done.3, bf16[5,512,128]{2,1,0:T(8,128)(2,1)} %copy-done.4, f32[5,512]{1,0:T(8,128)} %copy-done.5, ...), custom_call_target="tpu_custom_call" | custom-call | flops 429496729600 | bytes 419430400 | tf_op jit(solution)/shard_map/before/pallas_call | solution.py:282
  163.5 1.3 copy.33
  164.9 1.3 fusion.1
  166.2 170.3 %all-to-all-done.1.kv_ref = bf16[64,256,128]{2,1,0:T(8,128)(2,1)} async-done(((bf16[64,256,128]{2,1,0:T(8,128)(2,1)}), bf16[64,256,128]{2,1,0:T(8,128)(2,1)}, u32[]{:S(2)}, u32[]{:S(2)}) %all-to-all-start.1) | async-done | bytes 4194336 | tf_op jit(solution)/shard_map/all_to_all | solution.py:259
  336.4 10.7 %far.1 = bf16[512,8,128]{2,1,0:T(8,128)(2,1)} custom-call(s32[16]{0:T(128)} %reshape.38.flag_ref, bf16[8,512,128]{2,1,0:T(8,128)(2,1)} %get-tuple-element.15.q_ref, bf16[64,256,128]{2,1,0:T(8,128)(2,1)} %all-to-all-done.1.kv_ref, f32[8,512,128]{2,1,0:T(8,128)} %get-tuple-element.26.acc_ref, f32[8,512]{1,0:T(8,128)} %bitcast.11), custom_call_target="tpu_custom_call" | custom-call | flops 2147483648 | bytes 10485760 | tf_op jit(solution)/shard_map/far/pallas_call | solution.py:304
  (15 shorter events, 0.0 us)
Async XLA Ops:
  6.1 26.1 %collective-permute-start.1 = (bf16[2,3,512,128]{3,2,1,0:T(8,128)(2,1)}, bf16[2,3,512,128]{3,2,1,0:T(8,128)(2,1)S(1)}, u32[]{:S(2)}, u32[]{:S(2)}) collective-permute-start(bf16[2,3,512,128]{3,2,1,0:T(8,128)(2,1)} %get-tuple-element.18), channel_id=1, source_target_pairs={{0,8},{8,16},{16,24},{24,32},{32,40},{40,48},{48,56},{56,64},{64,7... | collective-permute-start | bytes 2359304 | tf_op jit(solution)/shard_map/ppermute | solution.py:220
  9.9 22.2 %collective-permute-start = (bf16[5,512,128]{2,1,0:T(8,128)(2,1)}, bf16[5,512,128]{2,1,0:T(8,128)(2,1)}, u32[]{:S(2)}, u32[]{:S(2)}) collective-permute-start(bf16[5,512,128]{2,1,0:T(8,128)(2,1)} %get-tuple-element.17), channel_id=1, source_target_pairs={{8,0},{16,8},{24,16},{32,24},{40,32},{48,40},{56,48},{64,56},{72,6... | collective-permute-start | bytes 1966088 | tf_op jit(solution)/shard_map/ppermute | solution.py:219
  11.2 20.7 %copy-start.2 = (s32[64,8,3]{0,1,2:T(8,128)S(1)}, s32[64,8,3]{0,1,2:T(8,128)}, u32[]{:S(2)}) copy-start(s32[64,8,3]{0,1,2:T(8,128)} %param.7) | copy-start | bytes 18436
  11.3 125.0 %all-to-all-start = ((bf16[64,136,128]{2,1,0:T(8,128)(2,1)}), bf16[64,136,128]{2,1,0:T(8,128)(2,1)S(1)}, u32[]{:S(2)}, u32[]{:S(2)}) async-start(bf16[64,136,128]{2,1,0:T(8,128)(2,1)} %get-tuple-element.16.kv_ref), calls=%async_computation | async-start | bytes 4456448 | tf_op jit(solution)/shard_map/all_to_all | solution.py:222
  32.2 6.6 %copy-start.3 = (bf16[2,3,512,128]{3,2,1,0:T(8,128)(2,1)}, bf16[2,3,512,128]{3,2,1,0:T(8,128)(2,1)S(1)}, u32[]{:S(2)}) copy-start(bf16[2,3,512,128]{3,2,1,0:T(8,128)(2,1)S(1)} %collective-permute-done.1.kv_ref) | copy-start | bytes 2359300
  38.7 111.3 %collective-permute-start.2 = (bf16[5,512,128]{2,1,0:T(8,128)(2,1)}, bf16[5,512,128]{2,1,0:T(8,128)(2,1)S(1)}, u32[]{:S(2)}, u32[]{:S(2)}) collective-permute-start(bf16[5,512,128]{2,1,0:T(8,128)(2,1)} %get-tuple-element.23), channel_id=1, source_target_pairs={{0,8},{8,16},{16,24},{24,32},{32,40},{40,48},{48,56},{56,64},{64,7... | collective-permute-start | bytes 1966088 | tf_op jit(solution)/shard_map/ppermute | solution.py:246
  46.5 103.5 %collective-permute-start.3 = (f32[5,512]{1,0:T(8,128)S(1)}, f32[5,512]{1,0:T(8,128)S(1)}, u32[]{:S(2)}, u32[]{:S(2)}) collective-permute-start(f32[5,512]{1,0:T(8,128)S(1)} %slice_bitcast_fusion), channel_id=1, source_target_pairs={{0,8},{8,16},{16,24},{24,32},{32,40},{40,48},{48,56},{56,64},{64,7... | collective-permute-start | bytes 30728 | tf_op jit(solution)/shard_map/ppermute | solution.py:247
  139.1 2.0 copy-start
  141.1 195.3 %all-to-all-start.1 = ((bf16[64,256,128]{2,1,0:T(8,128)(2,1)}), bf16[64,256,128]{2,1,0:T(8,128)(2,1)}, u32[]{:S(2)}, u32[]{:S(2)}) async-start(bf16[64,256,128]{2,1,0:T(8,128)(2,1)} %copy-done), calls=%async_computation.1 | async-start | bytes 8388608 | tf_op jit(solution)/shard_map/all_to_all | solution.py:259
  150.0 0.9 copy-start.5
  150.0 0.9 copy-start.4
  150.9 14.0 %copy-start.1 = (bf16[8,512,128]{2,1,0:T(8,128)(2,1)S(1)}, bf16[8,512,128]{2,1,0:T(8,128)(2,1)}, u32[]{:S(2)}) copy-start(bf16[8,512,128]{2,1,0:T(8,128)(2,1)} %get-tuple-element.15.q_ref) | copy-start | bytes 3145732
  150.9 14.0 %copy-start.6 = (pred[64]{0:T(512)(128)(4,1)S(1)}, pred[64]{0:T(512)(128)(4,1)}, u32[]{:S(2)}) copy-start(pred[64]{0:T(512)(128)(4,1)} %iota_compare_fusion) | copy-start | bytes 196

commit v5 on v4

--- a/solution.py
+++ b/solution.py
@@ -58,15 +58,17 @@
 
 
 def pick_kernel(table_ref, parts_ref, out_ref):
-    blocks = parts_ref.shape[0]
-    base = pl.program_id(0) * blocks * 2
+    count, rows, _ = out_ref.shape
+    base = pl.program_id(0) * count * (rows // ROWS)
 
     def one(c, carry):
-        out_ref[c, :ROWS] = parts_ref[table_ref[base + 2 * c]]
-        out_ref[c, ROWS:] = parts_ref[table_ref[base + 2 * c + 1]]
+        for item in range(rows // ROWS):
+            here = pl.ds(item // 2 * ROWS, ROWS)
+            picked = table_ref[base + c * (rows // ROWS) + item]
+            out_ref[c, item * ROWS : (item + 1) * ROWS] = parts_ref[picked, here]
         return carry
 
-    lax.fori_loop(0, blocks, one, 0, unroll=16)
+    lax.fori_loop(0, count, one, 0, unroll=True)
 
 
 def halves(x):
@@ -192,7 +194,7 @@
     by_head = functools.partial(jax.ShapeDtypeStruct, (heads, block_len, head_dim))
 
     given = 5
-    chunks = 4
+    chunks = 2
     tokens = block_len // chunks
     send, q, queries_back, rows_ahead = pl.pallas_call(
         pack_kernel,
@@ -225,7 +227,7 @@
     first = jnp.where(selection[:, :, 0] == owner - 1, selection[:, :, 1], selection[:, :, 0])
     last = jnp.where(selection[:, :, 2] == owner - 1, selection[:, :, 1], selection[:, :, 2])
     picks = jnp.stack([first, last], axis=2)
-    table = picks.transpose(1, 0, 2).reshape(-1)
+    table = picks.reshape(-1)
     mine = lax.dynamic_index_in_dim(picks, position, 0, keepdims=False)
     usable = (mine < position).astype(jnp.int32).reshape(-1)
 
@@ -247,12 +249,16 @@
     got_lse = lax.ppermute(gift_lse, "ctx", ahead)
     parts, _ = lax.optimization_barrier((parts, gift_lse))
 
+    some = blocks // 8
     picked = pl.pallas_call(
         pick_kernel,
         grid_spec=pltpu.PrefetchScalarGridSpec(
-            num_scalar_prefetch=1, grid=(heads,), in_specs=[piece], out_specs=pair
+            num_scalar_prefetch=1,
+            grid=(blocks // some,),
+            in_specs=[pl.BlockSpec(send.shape, lambda i, *_: (0, 0, 0))],
+            out_specs=pl.BlockSpec((some, heads * 2 * ROWS, head_dim), lambda i, *_: (i, 0, 0)),
         ),
-        out_shape=jax.ShapeDtypeStruct((blocks, heads * 2 * ROWS, head_dim), BF16),
+        out_shape=pltpu.HBM((blocks, heads * 2 * ROWS, head_dim), BF16),
         compiler_params=small,
         name="pick",
     )(table, parts)

time: 348 us -> 347 us (level)
  no operation moved by 1% of the time
where the time goes in v5:
time: 347 us; the launch traced here: 346 us
  waiting for transfers between devices  247 us (71%)
  Pallas kernels  48.3 us (14%)
  starting transfers between devices  41.4 us (12%)
  local copies, waits for them, and re-layouts  6.89 us (2%)
    all_to_all x1, waiting for transfers between devices, body(): lax.all_to_all(picked, 'ctx', split_axis=0, concat_axis=0, tiled=True)  170 us
    all_to_all x1, waiting for transfers between devices, body(): parts = lax.all_to_all(send, 'ctx', split_axis=0, concat_axis=0, tiled=True)  76.5 us
    all_to_all x1, starting transfers between devices, body(): parts = lax.all_to_all(send, 'ctx', split_axis=0, concat_axis=0, tiled=True)  20.6 us
    pallas_call x1, Pallas kernels, body(): pl.pallas_call(functools.partial(before_kernel, scale, given), grid_spec=...  12.7 us
    pallas_call x1, Pallas kernels, body(): pl.pallas_call(functools.partial(far_kernel, scale), grid_spec=pltpu.Pref...  10.7 us
    pallas_call x1, Pallas kernels, body(): pl.pallas_call(functools.partial(own_kernel, scale), grid=(heads,), in_sp...  9.09 us
    all_to_all x1, starting transfers between devices, body(): lax.all_to_all(picked, 'ctx', split_axis=0, concat_axis=0, tiled=True)  8.83 us
  transfers between devices with their start and end apart: 6, of which 2 were waited for; matrix products, arithmetic and copies ran while one was open for 2% of the time, Pallas kernels for 9%

profile of v5, /device:TPU:6, one launch (start us, length us, event | category | flops | bytes accessed | tf_op | source)
XLA Modules:
  0.0 346.1 jit_solution(12816932472078405751)
XLA Ops:
  0.6 4.7 %pack.1 = (bf16[64,136,128]{2,1,0:T(8,128)(2,1)}, bf16[8,512,128]{2,1,0:T(8,128)(2,1)}, bf16[5,512,128]{2,1,0:T(8,128)(2,1)}, bf16[2,3,512,128]{3,2,1,0:T(8,128)(2,1)}) custom-call(bf16[512,8,128]{2,1,0:T(8,128)(2,1)} %q_ref.1, bf16[512,8,128]{2,1,0:T(8,128)(2,1)} %k_ref.1, bf16[512,8,128]{2,1,0:T(8,128)(2,1)} %v_ref.1), custom_call_target="tpu_custom_call" | custom-call | tf_op jit(solution)/shard_map/pack/pallas_call | solution.py:199
  5.3 3.9 %collective-permute-start.1 = (bf16[2,3,512,128]{3,2,1,0:T(8,128)(2,1)}, bf16[2,3,512,128]{3,2,1,0:T(8,128)(2,1)S(1)}, u32[]{:S(2)}, u32[]{:S(2)}) collective-permute-start(bf16[2,3,512,128]{3,2,1,0:T(8,128)(2,1)} %get-tuple-element.18), channel_id=1, source_target_pairs={{0,8},{8,16},{16,24},{24,32},{32,40},{40,48},{48,56},{56,64},{64,7... | collective-permute-start | bytes 2359304 | tf_op jit(solution)/shard_map/ppermute | solution.py:222
  9.2 1.3 collective-permute-start
  10.5 0.0 copy-start.1
  10.5 20.6 %all-to-all-start = ((bf16[64,136,128]{2,1,0:T(8,128)(2,1)}), bf16[64,136,128]{2,1,0:T(8,128)(2,1)S(1)}, u32[]{:S(2)}, u32[]{:S(2)}) async-start(bf16[64,136,128]{2,1,0:T(8,128)(2,1)} %get-tuple-element.16.kv_ref), calls=%async_computation | async-start | bytes 4456448 | tf_op jit(solution)/shard_map/all_to_all | solution.py:224
  31.2 0.0 copy-done.1
  31.2 0.0 collective-permute-done.q_ref
  31.2 0.0 collective-permute-done.1.kv_ref
  31.2 0.0 copy-start.2
  31.2 6.5 %give.1 = (bf16[5,512,128]{2,1,0:T(8,128)(2,1)}, f32[5,512,128]{2,1,0:T(8,128)}) custom-call(bf16[5,512,128]{2,1,0:T(8,128)(2,1)} %collective-permute-done.q_ref, bf16[64,136,128]{2,1,0:T(8,128)(2,1)} %get-tuple-element.16.kv_ref), custom_call_target="tpu_custom_call" | custom-call | flops 107374182400 | bytes 104857600 | tf_op jit(solution)/shard_map/give/pallas_call | solution.py:234
  37.8 3.5 %collective-permute-start.2 = (bf16[5,512,128]{2,1,0:T(8,128)(2,1)}, bf16[5,512,128]{2,1,0:T(8,128)(2,1)S(1)}, u32[]{:S(2)}, u32[]{:S(2)}) collective-permute-start(bf16[5,512,128]{2,1,0:T(8,128)(2,1)} %get-tuple-element.23), channel_id=1, source_target_pairs={{0,8},{8,16},{16,24},{24,32},{32,40},{40,48},{48,56},{56,64},{64,7... | collective-permute-start | bytes 1966088 | tf_op jit(solution)/shard_map/ppermute | solution.py:248
  41.3 0.2 copy.23
  41.5 0.6 iota_compare_fusion
  42.1 2.9 copy.25
  45.0 0.7 slice_bitcast_fusion
  45.7 3.3 collective-permute-start.3
  49.1 9.1 %own.1 = (f32[8,512,128]{2,1,0:T(8,128)}, f32[8,512,128]{2,1,0:T(8,128)}) custom-call(bf16[8,512,128]{2,1,0:T(8,128)(2,1)} %get-tuple-element.15.q_ref, bf16[64,136,128]{2,1,0:T(8,128)(2,1)} %get-tuple-element.16.kv_ref), custom_call_target="tpu_custom_call" | custom-call | flops 1073741824 | bytes 6291456 | tf_op jit(solution)/shard_map/own/pallas_call | solution.py:272
  58.1 0.2 reshape.35.table_ref
  58.3 0.7 reshape.38.flag_ref
  59.0 76.5 %all-to-all-done.parts_ref = bf16[64,136,128]{2,1,0:T(8,128)(2,1)S(1)} async-done(((bf16[64,136,128]{2,1,0:T(8,128)(2,1)}), bf16[64,136,128]{2,1,0:T(8,128)(2,1)S(1)}, u32[]{:S(2)}, u32[]{:S(2)}) %all-to-all-start) | async-done | bytes 2228256 | tf_op jit(solution)/shard_map/all_to_all | solution.py:224
  135.5 4.6 %pick.1 = bf16[64,256,128]{2,1,0:T(8,128)(2,1)} custom-call(s32[1024]{0:T(1024)S(1)} %reshape.35.table_ref, bf16[64,136,128]{2,1,0:T(8,128)(2,1)S(1)} %all-to-all-done.parts_ref), custom_call_target="tpu_custom_call" | custom-call | tf_op jit(solution)/shard_map/pick/pallas_call | solution.py:253
  140.1 8.8 %all-to-all-start.1 = ((bf16[64,256,128]{2,1,0:T(8,128)(2,1)}), bf16[64,256,128]{2,1,0:T(8,128)(2,1)}, u32[]{:S(2)}, u32[]{:S(2)}) async-start(bf16[64,256,128]{2,1,0:T(8,128)(2,1)} %pick.1), calls=%async_computation.1 | async-start | bytes 8388608 | tf_op jit(solution)/shard_map/all_to_all | solution.py:265
  149.0 0.0 collective-permute-done.3.lse_ref
  149.0 0.0 copy-start.4
  149.0 0.0 collective-permute-done.2.got_ref
  149.0 0.9 copy-done.3
  149.9 12.7 %before.1 = (f32[8,512,128]{2,1,0:T(8,128)}, f32[8,1,512]{2,1,0:T(1,128)}) custom-call(s32[1]{0:T(128)} %bitcast.1.flag_ref, bf16[8,512,128]{2,1,0:T(8,128)(2,1)} %get-tuple-element.15.q_ref, bf16[2,3,512,128]{3,2,1,0:T(8,128)(2,1)} %copy-done.2, bf16[5,512,128]{2,1,0:T(8,128)(2,1)} %copy-done.3, f32[5,512]{1,0:T(8,128)} %copy-done.4, ...), custom_call_target="tpu_custom_call" | custom-call | flops 429496729600 | bytes 419430400 | tf_op jit(solution)/shard_map/before/pallas_call | solution.py:288
  162.5 1.3 copy.31
  163.9 0.0 copy-done
  163.9 1.3 fusion.1
  165.2 170.3 %all-to-all-done.1.kv_ref = bf16[64,256,128]{2,1,0:T(8,128)(2,1)} async-done(((bf16[64,256,128]{2,1,0:T(8,128)(2,1)}), bf16[64,256,128]{2,1,0:T(8,128)(2,1)}, u32[]{:S(2)}, u32[]{:S(2)}) %all-to-all-start.1) | async-done | bytes 4194336 | tf_op jit(solution)/shard_map/all_to_all | solution.py:265
  335.4 10.7 %far.1 = bf16[512,8,128]{2,1,0:T(8,128)(2,1)} custom-call(s32[16]{0:T(128)} %reshape.38.flag_ref, bf16[8,512,128]{2,1,0:T(8,128)(2,1)} %get-tuple-element.15.q_ref, bf16[64,256,128]{2,1,0:T(8,128)(2,1)} %all-to-all-done.1.kv_ref, f32[8,512,128]{2,1,0:T(8,128)} %get-tuple-element.26.acc_ref, f32[8,512]{1,0:T(8,128)} %bitcast.9), custom_call_target="tpu_custom_call" | custom-call | flops 2147483648 | bytes 10485760 | tf_op jit(solution)/shard_map/far/pallas_call | solution.py:310
  (11 shorter events, 0.0 us)
Async XLA Ops:
  5.3 25.9 %collective-permute-start.1 = (bf16[2,3,512,128]{3,2,1,0:T(8,128)(2,1)}, bf16[2,3,512,128]{3,2,1,0:T(8,128)(2,1)S(1)}, u32[]{:S(2)}, u32[]{:S(2)}) collective-permute-start(bf16[2,3,512,128]{3,2,1,0:T(8,128)(2,1)} %get-tuple-element.18), channel_id=1, source_target_pairs={{0,8},{8,16},{16,24},{24,32},{32,40},{40,48},{48,56},{56,64},{64,7... | collective-permute-start | bytes 2359304 | tf_op jit(solution)/shard_map/ppermute | solution.py:222
  9.2 22.0 %collective-permute-start = (bf16[5,512,128]{2,1,0:T(8,128)(2,1)}, bf16[5,512,128]{2,1,0:T(8,128)(2,1)}, u32[]{:S(2)}, u32[]{:S(2)}) collective-permute-start(bf16[5,512,128]{2,1,0:T(8,128)(2,1)} %get-tuple-element.17), channel_id=1, source_target_pairs={{8,0},{16,8},{24,16},{32,24},{40,32},{48,40},{56,48},{64,56},{72,6... | collective-permute-start | bytes 1966088 | tf_op jit(solution)/shard_map/ppermute | solution.py:221
  10.5 20.7 %copy-start.1 = (s32[64,8,3]{0,1,2:T(8,128)S(1)}, s32[64,8,3]{0,1,2:T(8,128)}, u32[]{:S(2)}) copy-start(s32[64,8,3]{0,1,2:T(8,128)} %param.7) | copy-start | bytes 18436
  10.5 125.0 %all-to-all-start = ((bf16[64,136,128]{2,1,0:T(8,128)(2,1)}), bf16[64,136,128]{2,1,0:T(8,128)(2,1)S(1)}, u32[]{:S(2)}, u32[]{:S(2)}) async-start(bf16[64,136,128]{2,1,0:T(8,128)(2,1)} %get-tuple-element.16.kv_ref), calls=%async_computation | async-start | bytes 4456448 | tf_op jit(solution)/shard_map/all_to_all | solution.py:224
  31.2 6.6 %copy-start.2 = (bf16[2,3,512,128]{3,2,1,0:T(8,128)(2,1)}, bf16[2,3,512,128]{3,2,1,0:T(8,128)(2,1)S(1)}, u32[]{:S(2)}) copy-start(bf16[2,3,512,128]{3,2,1,0:T(8,128)(2,1)S(1)} %collective-permute-done.1.kv_ref) | copy-start | bytes 2359300
  37.8 111.2 %collective-permute-start.2 = (bf16[5,512,128]{2,1,0:T(8,128)(2,1)}, bf16[5,512,128]{2,1,0:T(8,128)(2,1)S(1)}, u32[]{:S(2)}, u32[]{:S(2)}) collective-permute-start(bf16[5,512,128]{2,1,0:T(8,128)(2,1)} %get-tuple-element.23), channel_id=1, source_target_pairs={{0,8},{8,16},{16,24},{24,32},{32,40},{40,48},{48,56},{56,64},{64,7... | collective-permute-start | bytes 1966088 | tf_op jit(solution)/shard_map/ppermute | solution.py:248
  45.7 103.2 %collective-permute-start.3 = (f32[5,512]{1,0:T(8,128)S(1)}, f32[5,512]{1,0:T(8,128)S(1)}, u32[]{:S(2)}, u32[]{:S(2)}) collective-permute-start(f32[5,512]{1,0:T(8,128)S(1)} %slice_bitcast_fusion), channel_id=1, source_target_pairs={{0,8},{8,16},{16,24},{24,32},{32,40},{40,48},{48,56},{56,64},{64,7... | collective-permute-start | bytes 30728 | tf_op jit(solution)/shard_map/ppermute | solution.py:249
  140.1 195.3 %all-to-all-start.1 = ((bf16[64,256,128]{2,1,0:T(8,128)(2,1)}), bf16[64,256,128]{2,1,0:T(8,128)(2,1)}, u32[]{:S(2)}, u32[]{:S(2)}) async-start(bf16[64,256,128]{2,1,0:T(8,128)(2,1)} %pick.1), calls=%async_computation.1 | async-start | bytes 8388608 | tf_op jit(solution)/shard_map/all_to_all | solution.py:265
  149.0 0.9 copy-start.4
  149.0 0.9 copy-start.3
  149.9 14.0 %copy-start = (bf16[8,512,128]{2,1,0:T(8,128)(2,1)S(1)}, bf16[8,512,128]{2,1,0:T(8,128)(2,1)}, u32[]{:S(2)}) copy-start(bf16[8,512,128]{2,1,0:T(8,128)(2,1)} %get-tuple-element.15.q_ref) | copy-start | bytes 3145732
  149.9 14.0 %copy-start.5 = (pred[64]{0:T(512)(128)(4,1)S(1)}, pred[64]{0:T(512)(128)(4,1)}, u32[]{:S(2)}) copy-start(pred[64]{0:T(512)(128)(4,1)} %iota_compare_fusion) | copy-start | bytes 196

commit v6 on v5

--- a/solution.py
+++ b/solution.py
@@ -15,7 +15,7 @@
 BF16 = jnp.bfloat16
 
 
-def pack_kernel(q_ref, k_ref, v_ref, out_ref, qt_ref, back_ref, ahead_ref, total_ref):
+def pack_kernel(q_ref, k_ref, v_ref, out_ref, back_ref, ahead_ref, total_ref):
     tokens, heads, head_dim = k_ref.shape
     count = tokens // ROWS
     step, steps = pl.program_id(0), pl.num_programs(0)
@@ -30,7 +30,6 @@
         here = pl.ds(p * ROWS, ROWS)
         slot = step * count + p
         by_head = jnp.transpose(q_ref[here].astype(F32), (1, 0, 2)).astype(BF16)
-        qt_ref[:, here] = by_head
         back_ref[:, here] = by_head[:given]
         keys = k_ref[here].astype(F32)
         by_head = jnp.transpose(keys, (1, 0, 2)).astype(BF16)
@@ -196,26 +195,25 @@
     given = 5
     chunks = 2
     tokens = block_len // chunks
-    send, q, queries_back, rows_ahead = pl.pallas_call(
+    send, queries_back, rows_ahead = pl.pallas_call(
         pack_kernel,
         grid=(chunks,),
         in_specs=[pl.BlockSpec((tokens, heads, head_dim), lambda i: (i, 0, 0))] * 3,
         out_specs=[
             pl.BlockSpec((ctx_size, heads * (ROWS + 1), head_dim), lambda i: (0, 0, 0)),
-            pl.BlockSpec((heads, tokens, head_dim), lambda i: (0, i, 0)),
             pl.BlockSpec((given, tokens, head_dim), lambda i: (0, i, 0)),
             pl.BlockSpec((2, heads - given, tokens, head_dim), lambda i: (0, 0, i, 0)),
         ],
         scratch_shapes=[pltpu.VMEM((heads, head_dim), F32)],
         out_shape=[
             jax.ShapeDtypeStruct((ctx_size, heads * (ROWS + 1), head_dim), BF16),
-            by_head(BF16),
             jax.ShapeDtypeStruct((given, block_len, head_dim), BF16),
             jax.ShapeDtypeStruct((2, heads - given, block_len, head_dim), BF16),
         ],
         compiler_params=params,
         name="pack",
     )(queries, key_rows, value_rows)
+    q = queries.transpose(1, 0, 2)
     back = [(i + 1, i) for i in range(ctx_size - 1)]
     ahead = [(i, i + 1) for i in range(ctx_size - 1)]
     next_queries = lax.ppermute(queries_back, "ctx", back)

time: 347 us -> 347 us (level)
  transfers between devices with their start and end apart: 6 -> 6, of which waited for: 2 -> 2; matrix products, arithmetic and copies ran while one was open for 2% -> 3% of each run, Pallas kernels for 9% -> 9%
where the time goes in v6:
time: 347 us; the launch traced here: 346 us
  waiting for transfers between devices  246 us (71%)
  Pallas kernels  47.7 us (14%)
  starting transfers between devices  41.5 us (12%)
  local copies, waits for them, and re-layouts  7.95 us (2%)
    all_to_all x1, waiting for transfers between devices, body(): lax.all_to_all(picked, 'ctx', split_axis=0, concat_axis=0, tiled=True)  170 us
    all_to_all x1, waiting for transfers between devices, body(): parts = lax.all_to_all(send, 'ctx', split_axis=0, concat_axis=0, tiled=True)  75.8 us
    all_to_all x1, starting transfers between devices, body(): parts = lax.all_to_all(send, 'ctx', split_axis=0, concat_axis=0, tiled=True)  19.9 us
    pallas_call x1, Pallas kernels, body(): pl.pallas_call(functools.partial(before_kernel, scale, given), grid_spec=...  12.7 us
    pallas_call x1, Pallas kernels, body(): pl.pallas_call(functools.partial(far_kernel, scale), grid_spec=pltpu.Pref...  10.7 us
    pallas_call x1, Pallas kernels, body(): pl.pallas_call(functools.partial(own_kernel, scale), grid=(heads,), in_sp...  9.09 us
    all_to_all x1, starting transfers between devices, body(): lax.all_to_all(picked, 'ctx', split_axis=0, concat_axis=0, tiled=True)  8.72 us
  transfers between devices with their start and end apart: 6, of which 2 were waited for; matrix products, arithmetic and copies ran while one was open for 3% of the time, Pallas kernels for 9%

profile of v6, /device:TPU:6, one launch (start us, length us, event | category | flops | bytes accessed | tf_op | source)
XLA Modules:
  0.0 345.7 jit_solution(10858960501251230486)
XLA Ops:
  0.6 4.5 %pack.1 = (bf16[64,136,128]{2,1,0:T(8,128)(2,1)}, bf16[5,512,128]{2,1,0:T(8,128)(2,1)}, bf16[2,3,512,128]{3,2,1,0:T(8,128)(2,1)}) custom-call(bf16[512,8,128]{2,1,0:T(8,128)(2,1)} %q_ref.1, bf16[512,8,128]{2,1,0:T(8,128)(2,1)} %k_ref.1, bf16[512,8,128]{2,1,0:T(8,128)(2,1)} %v_ref.1), custom_call_target="tpu_custom_call" | custom-call | tf_op jit(solution)/shard_map/pack/pallas_call | solution.py:198
  5.1 4.7 %collective-permute-start.1 = (bf16[2,3,512,128]{3,2,1,0:T(8,128)(2,1)}, bf16[2,3,512,128]{3,2,1,0:T(8,128)(2,1)}, u32[]{:S(2)}, u32[]{:S(2)}) collective-permute-start(bf16[2,3,512,128]{3,2,1,0:T(8,128)(2,1)} %get-tuple-element.16), channel_id=1, source_target_pairs={{0,8},{8,16},{16,24},{24,32},{32,40},{40,48},{48,56},{56,64},{64,7... | collective-permute-start | bytes 2359304 | tf_op jit(solution)/shard_map/ppermute | solution.py:220
  9.8 1.3 collective-permute-start
  11.1 0.0 copy-start
  11.1 19.9 %all-to-all-start = ((bf16[64,136,128]{2,1,0:T(8,128)(2,1)}), bf16[64,136,128]{2,1,0:T(8,128)(2,1)S(1)}, u32[]{:S(2)}, u32[]{:S(2)}) async-start(bf16[64,136,128]{2,1,0:T(8,128)(2,1)} %get-tuple-element.14.kv_ref), calls=%async_computation | async-start | bytes 4456448 | tf_op jit(solution)/shard_map/all_to_all | solution.py:222
  31.0 0.0 copy-start.2
  31.1 1.2 copy.37
  32.2 0.0 collective-permute-done.q_ref
  32.3 0.0 collective-permute-done.1.kv_ref
  32.3 6.3 %give.1 = (bf16[5,512,128]{2,1,0:T(8,128)(2,1)}, f32[5,512,128]{2,1,0:T(8,128)}) custom-call(bf16[5,512,128]{2,1,0:T(8,128)(2,1)} %collective-permute-done.q_ref, bf16[64,136,128]{2,1,0:T(8,128)(2,1)} %get-tuple-element.14.kv_ref), custom_call_target="tpu_custom_call" | custom-call | flops 107374182400 | bytes 104857600 | tf_op jit(solution)/shard_map/give/pallas_call | solution.py:232
  38.5 3.5 %collective-permute-start.2 = (bf16[5,512,128]{2,1,0:T(8,128)(2,1)}, bf16[5,512,128]{2,1,0:T(8,128)(2,1)S(1)}, u32[]{:S(2)}, u32[]{:S(2)}) collective-permute-start(bf16[5,512,128]{2,1,0:T(8,128)(2,1)} %get-tuple-element.21), channel_id=1, source_target_pairs={{0,8},{8,16},{16,24},{24,32},{32,40},{40,48},{48,56},{56,64},{64,7... | collective-permute-start | bytes 1966088 | tf_op jit(solution)/shard_map/ppermute | solution.py:246
  42.1 0.2 copy.26
  42.2 0.5 iota_compare_fusion
  42.8 2.9 copy.29
  45.7 0.7 slice_bitcast_fusion
  46.4 3.3 collective-permute-start.3
  49.7 9.1 %own.1 = (f32[8,512,128]{2,1,0:T(8,128)}, f32[8,512,128]{2,1,0:T(8,128)}) custom-call(bf16[8,512,128]{2,1,0:T(8,128)(2,1)} %bitcast.12, bf16[64,136,128]{2,1,0:T(8,128)(2,1)} %get-tuple-element.14.kv_ref), custom_call_target="tpu_custom_call" | custom-call | flops 1073741824 | bytes 6291456 | tf_op jit(solution)/shard_map/own/pallas_call | solution.py:270
  58.8 0.2 reshape.35.table_ref
  59.0 0.6 reshape.38.flag_ref
  59.6 75.8 %all-to-all-done.parts_ref = bf16[64,136,128]{2,1,0:T(8,128)(2,1)S(1)} async-done(((bf16[64,136,128]{2,1,0:T(8,128)(2,1)}), bf16[64,136,128]{2,1,0:T(8,128)(2,1)S(1)}, u32[]{:S(2)}, u32[]{:S(2)}) %all-to-all-start) | async-done | bytes 2228256 | tf_op jit(solution)/shard_map/all_to_all | solution.py:222
  135.4 4.6 %pick.1 = bf16[64,256,128]{2,1,0:T(8,128)(2,1)} custom-call(s32[1024]{0:T(1024)S(1)} %reshape.35.table_ref, bf16[64,136,128]{2,1,0:T(8,128)(2,1)S(1)} %all-to-all-done.parts_ref), custom_call_target="tpu_custom_call" | custom-call | tf_op jit(solution)/shard_map/pick/pallas_call | solution.py:251
  140.0 8.7 %all-to-all-start.1 = ((bf16[64,256,128]{2,1,0:T(8,128)(2,1)}), bf16[64,256,128]{2,1,0:T(8,128)(2,1)}, u32[]{:S(2)}, u32[]{:S(2)}) async-start(bf16[64,256,128]{2,1,0:T(8,128)(2,1)} %pick.1), calls=%async_computation.1 | async-start | bytes 8388608 | tf_op jit(solution)/shard_map/all_to_all | solution.py:263
  148.7 0.0 copy-start.4
  148.7 0.0 collective-permute-done.2.got_ref
  148.7 0.0 copy-start.3
  148.8 0.6 copy-done.4
  149.3 0.3 copy-done.3
  149.6 12.7 %before.1 = (f32[8,512,128]{2,1,0:T(8,128)}, f32[8,1,512]{2,1,0:T(1,128)}) custom-call(s32[1]{0:T(128)} %bitcast.2.flag_ref, bf16[8,512,128]{2,1,0:T(8,128)(2,1)} %bitcast.13, bf16[2,3,512,128]{3,2,1,0:T(8,128)(2,1)} %collective-permute-done.1.kv_ref, bf16[5,512,128]{2,1,0:T(8,128)(2,1)} %copy-done.3, f32[5,512]{1,0:T(8,128)} %copy-done.4, ...), custom_call_target="tpu_custom_call" | custom-call | flops 429496729600 | bytes 419430400 | tf_op jit(solution)/shard_map/before/pallas_call | solution.py:286
  162.2 1.3 copy.38
  163.6 1.3 fusion.1
  164.9 170.1 %all-to-all-done.1.kv_ref = bf16[64,256,128]{2,1,0:T(8,128)(2,1)} async-done(((bf16[64,256,128]{2,1,0:T(8,128)(2,1)}), bf16[64,256,128]{2,1,0:T(8,128)(2,1)}, u32[]{:S(2)}, u32[]{:S(2)}) %all-to-all-start.1) | async-done | bytes 4194336 | tf_op jit(solution)/shard_map/all_to_all | solution.py:263
  335.0 10.7 %far.1 = bf16[512,8,128]{2,1,0:T(8,128)(2,1)} custom-call(s32[16]{0:T(128)} %reshape.38.flag_ref, bf16[8,512,128]{2,1,0:T(8,128)(2,1)} %bitcast.14, bf16[64,256,128]{2,1,0:T(8,128)(2,1)} %all-to-all-done.1.kv_ref, f32[8,512,128]{2,1,0:T(8,128)} %get-tuple-element.24.acc_ref, f32[8,512]{1,0:T(8,128)} %bitcast.15), custom_call_target="tpu_custom_call" | custom-call | flops 2147483648 | bytes 10485760 | tf_op jit(solution)/shard_map/far/pallas_call | solution.py:308
  (12 shorter events, 0.0 us)
Async XLA Ops:
  5.1 27.2 %collective-permute-start.1 = (bf16[2,3,512,128]{3,2,1,0:T(8,128)(2,1)}, bf16[2,3,512,128]{3,2,1,0:T(8,128)(2,1)}, u32[]{:S(2)}, u32[]{:S(2)}) collective-permute-start(bf16[2,3,512,128]{3,2,1,0:T(8,128)(2,1)} %get-tuple-element.16), channel_id=1, source_target_pairs={{0,8},{8,16},{16,24},{24,32},{32,40},{40,48},{48,56},{56,64},{64,7... | collective-permute-start | bytes 2359304 | tf_op jit(solution)/shard_map/ppermute | solution.py:220
  9.8 22.4 %collective-permute-start = (bf16[5,512,128]{2,1,0:T(8,128)(2,1)}, bf16[5,512,128]{2,1,0:T(8,128)(2,1)}, u32[]{:S(2)}, u32[]{:S(2)}) collective-permute-start(bf16[5,512,128]{2,1,0:T(8,128)(2,1)} %get-tuple-element.15), channel_id=1, source_target_pairs={{8,0},{16,8},{24,16},{32,24},{40,32},{48,40},{56,48},{64,56},{72,6... | collective-permute-start | bytes 1966088 | tf_op jit(solution)/shard_map/ppermute | solution.py:219
  11.1 20.0 %copy-start = (bf16[512,8,128]{2,1,0:T(8,128)(2,1)S(1)}, bf16[512,8,128]{2,1,0:T(8,128)(2,1)}, u32[]{:S(2)}) copy-start(bf16[512,8,128]{2,1,0:T(8,128)(2,1)} %q_ref.1) | copy-start | bytes 3145732
  11.1 124.3 %all-to-all-start = ((bf16[64,136,128]{2,1,0:T(8,128)(2,1)}), bf16[64,136,128]{2,1,0:T(8,128)(2,1)S(1)}, u32[]{:S(2)}, u32[]{:S(2)}) async-start(bf16[64,136,128]{2,1,0:T(8,128)(2,1)} %get-tuple-element.14.kv_ref), calls=%async_computation | async-start | bytes 4456448 | tf_op jit(solution)/shard_map/all_to_all | solution.py:222
  31.0 1.2 copy-start.2
  38.5 110.2 %collective-permute-start.2 = (bf16[5,512,128]{2,1,0:T(8,128)(2,1)}, bf16[5,512,128]{2,1,0:T(8,128)(2,1)S(1)}, u32[]{:S(2)}, u32[]{:S(2)}) collective-permute-start(bf16[5,512,128]{2,1,0:T(8,128)(2,1)} %get-tuple-element.21), channel_id=1, source_target_pairs={{0,8},{8,16},{16,24},{24,32},{32,40},{40,48},{48,56},{56,64},{64,7... | collective-permute-start | bytes 1966088 | tf_op jit(solution)/shard_map/ppermute | solution.py:246
  46.4 102.3 %collective-permute-start.3 = (f32[5,512]{1,0:T(8,128)S(1)}, f32[5,512]{1,0:T(8,128)S(1)}, u32[]{:S(2)}, u32[]{:S(2)}) collective-permute-start(f32[5,512]{1,0:T(8,128)S(1)} %slice_bitcast_fusion), channel_id=1, source_target_pairs={{0,8},{8,16},{16,24},{24,32},{32,40},{40,48},{48,56},{56,64},{64,7... | collective-permute-start | bytes 30728 | tf_op jit(solution)/shard_map/ppermute | solution.py:247
  140.0 195.0 %all-to-all-start.1 = ((bf16[64,256,128]{2,1,0:T(8,128)(2,1)}), bf16[64,256,128]{2,1,0:T(8,128)(2,1)}, u32[]{:S(2)}, u32[]{:S(2)}) async-start(bf16[64,256,128]{2,1,0:T(8,128)(2,1)} %pick.1), calls=%async_computation.1 | async-start | bytes 8388608 | tf_op jit(solution)/shard_map/all_to_all | solution.py:263
  148.7 0.6 copy-start.4
  148.7 0.8 copy-start.3
  149.6 14.0 %copy-start.1 = (bf16[512,8,128]{2,1,0:T(8,128)(2,1)S(1)}, bf16[512,8,128]{2,1,0:T(8,128)(2,1)}, u32[]{:S(2)}) copy-start(bf16[512,8,128]{2,1,0:T(8,128)(2,1)} %q_ref.1) | copy-start | bytes 3145732
  149.6 14.0 %copy-start.5 = (pred[64]{0:T(512)(128)(4,1)S(1)}, pred[64]{0:T(512)(128)(4,1)}, u32[]{:S(2)}) copy-start(pred[64]{0:T(512)(128)(4,1)} %iota_compare_fusion) | copy-start | bytes 196
